TPU v7x, 32 devices: a whole 2x2x4 slice. The times are simulated.
32 devices in a mesh: pp: 4 (over y, core), node: 2 (over x), local: 4 (over z).
Axes of the slice: x: 2, y: 2, z: 4, core: 2. Of those that a mesh axis runs over, the one named last changes fastest.
Arguments:
- act_fwd: bfloat16 [4, 1024, 4096], P('pp', ('node', 'local')), may hold values from -6 to 6
- routes_fwd: int32 [4, 1024, 1], P('pp', ('node', 'local')), may hold values from 0 to 1; in each aligned block of 128 rows (0 to 127, 128 to 255, ..., all dimensions but the last counted through in order) at most 80 rows name the same one
- weight_fwd: float32 [4, 1024], P('pp', ('node', 'local')), may hold values from 0.25 to 1
- grad_bwd: bfloat16 [4, 1024, 4096], P('pp', ('node', 'local')), may hold values from -6 to 6
- routes_bwd: int32 [4, 1024, 1], P('pp', ('node', 'local')), may hold values from 0 to 1; in each aligned block of 128 rows (0 to 127, 128 to 255, ..., all dimensions but the last counted through in order) at most 80 rows name the same one
- weight_bwd: float32 [4, 1024], P('pp', ('node', 'local')), may hold values from 0.25 to 1
- saved_bwd: bfloat16 [4, 1024, 2048], P('pp', ('node', 'local')), may hold values from -8 to 8
- w_gate_up: bfloat16 [4, 2, 4096, 2048], P('pp', 'node', 'local'), may hold values from -0.09375 to 0.09375
- w_down: bfloat16 [4, 2, 1024, 4096], P('pp', 'node', None, 'local'), may hold values from -0.1875 to 0.1875
Outputs:
- next_input: bfloat16 [4, 1024, 4096], P('pp', ('node', 'local'))
- prev_grad: bfloat16 [4, 1024, 4096], P('pp', ('node', 'local'))
Inputs may be any that keep to these rules, and one draw needn't show every extreme that they name: `routes_fwd`: within each device's 128 tokens (aligned blocks of rows), no expert is named more than 80 times, a bound that some block reaches. `routes_bwd`: within each device's 128 tokens (aligned blocks of rows), no expert is named more than 80 times, a bound that some block reaches.
All inputs are finite; a program needn't handle non-finite values.
Results may differ from a plain program's by a relative error of at most 0.017.
Values may be sent and summed in bfloat16 or wider, within the bound.
No kernel may reach another device: no remote copies, remote signals or barrier semaphores. Data moves between devices by JAX's collectives and lax.ppermute only.
A program may use at most 128 MiB of HBM per device.

v0:
```python
import jax
import jax.numpy as jnp
from jax import lax
from jax.experimental import pallas as pl
from jax.experimental.pallas import tpu as pltpu
from jax.sharding import PartitionSpec as P

F32 = jnp.float32
BF16 = jnp.bfloat16
AXES = ("pp", "node", "local")


def move(value, by_pp=0, by_node=0, by_local=0, wrap=True, first=0, last=None):
    pps, nodes, locs = (lax.axis_size(a) for a in AXES)
    last = locs - 1 if last is None else last
    pairs = []
    for s in range(pps):
        for n in range(nodes):
            for l in range(locs):
                to = l + by_local
                if not wrap and not (first <= l <= last and 0 <= to < locs):
                    continue
                source = (s * nodes + n) * locs + l
                target = (((s + by_pp) % pps) * nodes + (n ^ by_node)) * locs + to % locs
                pairs.append((source, target))
    return lax.ppermute(value, AXES, pairs)


def sorted_places(route):
    ones = route.astype(F32)
    count = route.shape[0]
    earlier = (jnp.arange(count)[None, :] < jnp.arange(count)[:, None]).astype(F32)
    ones_before = jnp.dot(earlier, ones[:, None], preferred_element_type=F32)[:, 0]
    zeros = count - jnp.sum(ones)
    index = jnp.arange(count, dtype=F32)
    place = jnp.where(route == 0, index - ones_before, zeros + ones_before)
    return place.astype(jnp.int32)


def sorter(route):
    place = sorted_places(route)
    rows = jnp.arange(route.shape[0], dtype=jnp.int32)
    return (rows[:, None] == place[None, :]).astype(BF16)


def one_hot(row, count):
    return (row[:, None] == jnp.arange(count, dtype=jnp.int32)[None, :]).astype(BF16)


def dot_t(left, right):
    return lax.dot_general(left, right, (((1,), (1,)), ((), ())), preferred_element_type=F32)


def windows(blocks, node, capacity):
    tokens = blocks.shape[-2]
    start = tokens - capacity
    low = lax.slice_in_dim(blocks, 0, capacity, axis=-2 + blocks.ndim)
    high = lax.slice_in_dim(blocks, start, tokens, axis=-2 + blocks.ndim)
    own = jnp.where(node == 0, low, high)
    other = jnp.where(node == 0, high, low)
    return own, other


def join(*values):
    return lax.optimization_barrier(values)


def after(values, *others):
    return list(join(*values, *others)[: len(values)])


def cut(tokens, placer, local):
    column = tokens.shape[1] // 4
    blocks = []
    for m in range(4):
        block = lax.dynamic_slice_in_dim(tokens, ((local - m) % 4) * column, column, axis=1)
        blocks.append(jnp.dot(placer, block, preferred_element_type=F32).astype(BF16))
    return blocks


def sums(partial):
    right, left = partial(3), partial(1)
    for step in (1, 2, 3):
        right, left = right.astype(BF16), left.astype(BF16)
        got_r, got_l = yield (
            (right, dict(by_local=1, wrap=False, last=step - 1)),
            (left, dict(by_local=-1, wrap=False, first=4 - step)),
        )
        right = partial(3 - step).astype(F32) + got_r.astype(F32)
        if step < 3:
            left = partial(step + 1).astype(F32) + got_l.astype(F32)
    yield right + got_l.astype(F32)


def gathers(rows, local):
    from_left, from_right = [rows], [rows]
    for step in (1, 2, 3):
        got_r, got_l = yield (
            (from_left[-1], dict(by_local=1, wrap=False, first=step - 1)),
            (from_right[-1], dict(by_local=-1, wrap=False, last=4 - step)),
        )
        from_left.append(got_r)
        from_right.append(got_l)
    slots = [rows]
    for m in (1, 2, 3):
        slots.append(jnp.where(local + m < 4, from_right[m], from_left[4 - m]))
    yield jnp.stack(slots)


def send(pieces):
    return [move(value, **how) for value, how in pieces]


def operands(pieces):
    return [value for value, _ in pieces]


def valid(zeros, node, tokens, capacity):
    row = jnp.arange(capacity, dtype=F32)[None, :]
    return jnp.where(node == 0, row < zeros[:, None], row + (tokens - capacity) >= zeros[:, None])


def merge(own, other, node, tokens):
    slots, capacity, column = own.shape
    low = jnp.where(node == 0, own, other)
    high = jnp.where(node == 0, other, own)
    rest = jnp.zeros((slots, tokens - capacity, column), own.dtype)
    return jnp.concatenate([low, rest], axis=1) + jnp.concatenate([rest, high], axis=1)


def homeward(merged, by_pp):
    return [(merged[m], dict(by_pp=by_pp, by_local=m)) for m in (2, 1, 3, 0)]


def finish_kernel(at_ref, residual_ref, weight_ref, pick_ref, *refs):
    *blocks, out_ref, rows, sem = refs
    count = len(blocks)
    column = rows.shape[-1]
    copies = [pltpu.make_async_copy(blocks[i], rows.at[i], sem.at[i]) for i in range(count)]
    for copy in copies:
        copy.start()
    for i in range(count):
        copies[i].wait()
        cols = pl.ds(pl.multiple_of(at_ref[i] * column, column), column)
        moe = jnp.dot(pick_ref[...], rows[i], preferred_element_type=F32)
        total = residual_ref[:, cols].astype(F32) + weight_ref[...] * moe
        out_ref[0, :, cols] = total.astype(out_ref.dtype)


def finish(residual, weight, place, blocks, at):
    column = blocks[0].shape[-1]
    tokens, features = residual.shape
    vmem = pl.BlockSpec(memory_space=pltpu.VMEM)
    anywhere = pl.BlockSpec(memory_space=pl.ANY)
    return pl.pallas_call(
        finish_kernel,
        out_shape=jax.ShapeDtypeStruct((1, tokens, features), BF16),
        in_specs=[pl.BlockSpec(memory_space=pltpu.SMEM)] + [vmem] * 3 + [anywhere] * len(blocks),
        out_specs=vmem,
        scratch_shapes=[
            pltpu.VMEM((len(blocks), tokens, column), BF16),
            pltpu.SemaphoreType.DMA((len(blocks),)),
        ],
        compiler_params=pltpu.CompilerParams(vmem_limit_bytes=8 * 2**20),
        name="finish",
    )(at, residual, weight[:, None], one_hot(place, tokens), *blocks)


def body_pair(
    act_fwd, routes_fwd, weight_fwd, grad_bwd, routes_bwd, weight_bwd, saved_bwd, w_gate_up, w_down
):
    node = lax.axis_index("node")
    local = lax.axis_index("local")
    tokens_here = act_fwd.shape[1]
    capacity = 5 * tokens_here // 8
    w_gu = w_gate_up[0, 0]
    w_dn = w_down[0, 0]
    hidden_units = w_dn.shape[0]
    shape = (4, 2, capacity)

    act, grad = act_fwd[0], grad_bwd[0]
    route_a, route_b = routes_fwd[0, :, 0], routes_bwd[0, :, 0]
    sort_a, sort_b = sorter(route_a), sorter(route_b)
    zeros = tokens_here - jnp.stack([jnp.sum(route_a), jnp.sum(route_b)]).astype(F32)

    def in_rows(cuts, got):
        return windows(jnp.stack([cuts[0], got[1], got[0], got[2]]), node, capacity)

    def by_node(own, got, axis):
        return jnp.stack([jnp.where(node == 0, own, got), jnp.where(node == 0, got, own)], axis=axis)

    def split(done):
        own = lax.dynamic_index_in_dim(done, node, axis=1, keepdims=False)
        other = lax.dynamic_index_in_dim(done, 1 - node, axis=1, keepdims=False)
        return own, other

    def turn(chain, back, *others):
        pieces = chain.send(after(back, *others))
        return operands(pieces), send(pieces)

    dy = (weight_bwd[0][:, None] * grad.astype(F32)).astype(BF16)
    cut_b = cut(dy, sort_b, local)
    got_b = [move(cut_b[m], by_local=-m) for m in (2, 1, 3)]
    saved = jnp.dot(sort_b, saved_bwd[0], preferred_element_type=F32).astype(BF16)
    saved_own, saved_other = windows(saved, node, capacity)
    saved_got = move(saved_other, by_node=1)
    (zeros_wait,) = after([zeros], saved_other)
    zeros_got = move(zeros_wait, by_node=1)
    cut_a = cut(act, sort_a, local)
    *got_b, saved_got, zeros_got, a0, a1, a2, a3 = join(*got_b, saved_got, zeros_got, *cut_a)
    cut_a = [a0, a1, a2, a3]
    zeros = by_node(zeros, zeros_got, 0)
    got_a = [move(cut_a[m], by_local=-m) for m in (2, 1, 3)]
    own_b, other_b = in_rows(cut_b, got_b)
    column = own_b.shape[-1]
    got_bx = move(other_b, by_node=1)

    rows_b = by_node(own_b, got_bx, 1).reshape(-1, column)
    part_b = dot_t(rows_b, w_dn).astype(BF16).reshape(shape + (hidden_units,))
    chain_b = sums(lambda slot: part_b[slot])
    back_b = send(next(chain_b))
    *back_b, g0, g1, g2 = join(*back_b, *got_a)
    own_a, other_a = in_rows(cut_a, [g0, g1, g2])
    got_ax = move(other_a, by_node=1)
    act_next = move(after([act], other_a)[0], by_pp=1)
    values_b, back_b = turn(chain_b, back_b)
    values_b, back_b = turn(chain_b, back_b)
    *back_b, got_ax, act_next = join(*back_b, got_ax, act_next)
    dh = chain_b.send(back_b)
    dh = jnp.where(valid(zeros[:, 1], node, tokens_here, capacity)[..., None], dh, 0.0)
    saved_rows = by_node(saved_own, saved_got, 0)
    g = saved_rows[..., :hidden_units].astype(F32)
    u = saved_rows[..., hidden_units:].astype(F32)
    q = 1.0 / (1.0 + jnp.exp(-g))
    grad_gu = jnp.concatenate([dh * u * q * (1.0 + g * (1.0 - q)), dh * g * q], axis=-1).astype(
        BF16
    )

    chain_b = gathers(grad_gu, local)
    back_b = send(next(chain_b))
    grad_wait, route_wait, small_wait = after(
        [grad, route_b, jnp.stack([route_a.astype(F32), weight_fwd[0]])], grad_gu
    )
    grad_next = move(grad_wait, by_pp=-1)
    route_b_next = move(route_wait, by_pp=-1)
    small_next = move(small_wait, by_pp=1)
    rows_a = by_node(own_a, got_ax, 1).reshape(-1, column)
    part_a = jnp.dot(rows_a, w_gu, preferred_element_type=F32).astype(BF16)
    *back_b, part_a, grad_next, route_b_next, small_next = join(
        *back_b, part_a, grad_next, route_b_next, small_next
    )
    part_a = part_a.reshape(shape + (2 * hidden_units,))
    chain_a = sums(lambda slot: part_a[slot])
    values_b, back_b = turn(chain_b, back_b)
    back_a = send(next(chain_a))
    values_b, back_b = turn(chain_b, back_b)
    values_a, back_a = turn(chain_a, back_a)
    values_a, back_a = turn(chain_a, back_a)
    all_gu = chain_b.send(back_b)
    done_b = dot_t(all_gu.reshape(-1, 2 * hidden_units), w_gu).astype(BF16)
    own_b, other_b = split(done_b.reshape(shape + (column,)))
    got_b = move(other_b, by_node=1)
    *back_a, got_b = join(*back_a, got_b)

    preact = chain_a.send(back_a)
    preact = jnp.where(valid(zeros[:, 0], node, tokens_here, capacity)[..., None], preact, 0.0)
    hidden = (jax.nn.silu(preact[..., :hidden_units]) * preact[..., hidden_units:]).astype(BF16)
    all_hidden = [move(hidden, by_local=-m) for m in (1, 2, 3)]
    merged_b = merge(own_b, got_b, node, tokens_here)
    h1, h2, h3, merged_b = join(*all_hidden, merged_b)
    all_hidden = jnp.stack([hidden, h1, h2, h3])
    home_b = send(homeward(merged_b, -1))
    done_a = jnp.dot(
        all_hidden.reshape(-1, hidden_units), w_dn, preferred_element_type=F32
    ).astype(BF16)
    own_a, other_a = split(done_a.reshape(shape + (column,)))
    got_a = move(other_a, by_node=1)
    home_a = send(homeward(merge(own_a, got_a, node, tokens_here), 1))

    at = jnp.stack([(local - m) % 4 for m in (2, 1, 3, 0)]).astype(jnp.int32)
    ones = jnp.ones((tokens_here,), F32)
    prev_grad = finish(grad_next, ones, sorted_places(route_b_next), home_b, at)
    place_a = sorted_places(small_next[0].astype(jnp.int32))
    next_input = finish(act_next, small_next[1], place_a, home_a, at)
    return next_input, prev_grad


def from_behind(value, axis, by):
    length = lax.axis_size(axis)
    return lax.ppermute(value, axis, [(i, (i + by) % length) for i in range(length)])


def place_matrix(route, expert_count, capacity):
    onehot = (route[:, None] == jnp.arange(expert_count, dtype=jnp.int32)[None, :]).astype(
        jnp.int32
    )
    before = jnp.cumsum(onehot, axis=0) - onehot
    slot_index = jnp.sum(before * onehot, axis=1)
    target = route * capacity + slot_index
    positions = jnp.arange(expert_count * capacity, dtype=jnp.int32)
    return (positions[:, None] == target[None, :]).astype(jnp.bfloat16)


def pack_rows(placer, values, expert_count, capacity):
    packed = jnp.dot(placer, values, preferred_element_type=jnp.float32).astype(jnp.bfloat16)
    return packed.reshape(expert_count, capacity, values.shape[1])


def unpack_rows(placer, packed):
    flattened = packed.reshape(-1, packed.shape[-1])
    result = lax.dot_general(
        placer, flattened, (((0,), (0,)), ((), ())), preferred_element_type=jnp.float32
    )
    return result.astype(jnp.bfloat16)


def flat_outgoing(packed, local_count):
    expert_count, capacity, feature_count = packed.shape
    column = feature_count // local_count
    outgoing = packed.reshape(expert_count, capacity, local_count, column).transpose(0, 2, 1, 3)
    return outgoing.reshape(expert_count * local_count, capacity, column)


def flat_layout(received, expert_count, local_count):
    capacity = received.shape[1]
    column = received.shape[2]
    rows_in = received.reshape(expert_count, local_count, capacity, column).transpose(1, 0, 2, 3)
    return rows_in.reshape(-1, column)


def send_rows(packs, local_count):
    expert_count = packs[0].shape[0]
    outgoing = tuple((flat_outgoing(packed, local_count) for packed in packs))
    received = (
        lax.all_to_all(outgoing[0], ("node", "local"), split_axis=0, concat_axis=0, tiled=True),
        lax.all_to_all(outgoing[1], ("node", "local"), split_axis=0, concat_axis=0, tiled=True),
    )
    return tuple((flat_layout(item, expert_count, local_count) for item in received))


def return_rows(finished_pair, expert_count, capacity, local_count):
    column = finished_pair[0].shape[1]
    blocks = tuple(
        (item.reshape(local_count, expert_count, capacity, column) for item in finished_pair)
    )
    outgoing = tuple(
        (
            item.transpose(1, 0, 2, 3).reshape(expert_count * local_count, capacity, column)
            for item in blocks
        )
    )
    received = (
        lax.all_to_all(outgoing[0], ("node", "local"), split_axis=0, concat_axis=0, tiled=True),
        lax.all_to_all(outgoing[1], ("node", "local"), split_axis=0, concat_axis=0, tiled=True),
    )
    results = []
    for item in received:
        arranged = item.reshape(expert_count, local_count, capacity, column).transpose(0, 2, 1, 3)
        results.append(arranged.reshape(expert_count, capacity, local_count * column))
    return tuple(results)


def body(
    act_fwd, routes_fwd, weight_fwd, grad_bwd, routes_bwd, weight_bwd, saved_bwd, w_gate_up, w_down
):
    node_count = lax.axis_size("node")
    local_count = lax.axis_size("local")
    tokens_here = act_fwd.shape[1]
    capacity = 5 * tokens_here // (4 * node_count)
    rows_each = node_count * capacity
    w_gu = w_gate_up[0, 0]
    w_dn = w_down[0, 0]
    hidden_units = w_dn.shape[0]
    tokens_a = act_fwd[0]
    placer_a = place_matrix(routes_fwd[0, :, 0], node_count, capacity)
    cotangent = grad_bwd[0]
    placer_b = place_matrix(routes_bwd[0, :, 0], node_count, capacity)
    scaled = (weight_bwd[0][:, None] * cotangent.astype(jnp.float32)).astype(jnp.bfloat16)
    packed_a = pack_rows(placer_a, tokens_a, node_count, capacity)
    packed_b = pack_rows(placer_b, scaled, node_count, capacity)
    rows_a, rows_b = send_rows((packed_a, packed_b), local_count)
    saved_packed = pack_rows(placer_b, saved_bwd[0], node_count, capacity)
    saved_rows = lax.all_to_all(
        saved_packed, "node", split_axis=0, concat_axis=0, tiled=True
    ).reshape(rows_each, -1)
    row_block = rows_a
    preact = lax.psum_scatter(
        jnp.dot(row_block, w_gu, preferred_element_type=jnp.float32).astype(jnp.bfloat16),
        "local",
        scatter_dimension=0,
        tiled=True,
    ).astype(jnp.float32)
    row_block = rows_b
    grad_hidden = lax.psum_scatter(
        lax.dot_general(
            row_block, w_dn, (((1,), (1,)), ((), ())), preferred_element_type=jnp.float32
        ).astype(jnp.bfloat16),
        "local",
        scatter_dimension=0,
        tiled=True,
    ).astype(jnp.float32)
    hidden = (jax.nn.silu(preact[:, :hidden_units]) * preact[:, hidden_units:]).astype(jnp.bfloat16)
    done_a = jnp.dot(
        lax.all_gather(hidden, "local", axis=0, tiled=True),
        w_dn,
        preferred_element_type=jnp.float32,
    ).astype(jnp.bfloat16)
    gate_pre = saved_rows[:, :hidden_units].astype(jnp.float32)
    up_pre = saved_rows[:, hidden_units:].astype(jnp.float32)
    sigmoid_g = 1.0 / (1.0 + jnp.exp(-gate_pre))
    grad_gate = grad_hidden * up_pre * sigmoid_g * (1.0 + gate_pre * (1.0 - sigmoid_g))
    grad_up = grad_hidden * gate_pre * sigmoid_g
    grad_gu = jnp.concatenate([grad_gate, grad_up], axis=1).astype(jnp.bfloat16)
    product = lax.dot_general(
        lax.all_gather(grad_gu, "local", axis=0, tiled=True),
        w_gu,
        (((1,), (1,)), ((), ())),
        preferred_element_type=jnp.float32,
    )
    done_b = product.astype(jnp.bfloat16)
    back_a, back_b = return_rows((done_a, done_b), node_count, capacity, local_count)
    moe_a = unpack_rows(placer_a, back_a)
    result_a = tokens_a.astype(jnp.float32) + weight_fwd[0][:, None] * moe_a.astype(jnp.float32)
    result_a = result_a.astype(jnp.bfloat16)
    moe_b = unpack_rows(placer_b, back_b)
    result_b = (cotangent.astype(jnp.float32) + moe_b.astype(jnp.float32)).astype(jnp.bfloat16)
    next_input = from_behind(result_a[None], "pp", 1)
    prev_grad = from_behind(result_b[None], "pp", -1)
    return (next_input, prev_grad)


def solution(mesh):
    in_specs = (
        P("pp", ("node", "local"), None),
        P("pp", ("node", "local"), None),
        P("pp", ("node", "local")),
        P("pp", ("node", "local"), None),
        P("pp", ("node", "local"), None),
        P("pp", ("node", "local")),
        P("pp", ("node", "local"), None),
        P("pp", "node", "local", None),
        P("pp", "node", None, "local"),
    )
    out_specs = (P("pp", ("node", "local"), None), P("pp", ("node", "local"), None))
    paired = mesh.shape["node"] == 2 and mesh.shape["local"] == 4
    plan = body_pair if paired else body
    return jax.shard_map(plan, mesh=mesh, in_specs=in_specs, out_specs=out_specs, check_vma=False)
```

profile of v0, /device:TPU:0, one launch (start us, length us, event | category | flops | bytes accessed | tf_op | source)
XLA Modules:
  0.0 268.7 jit_solution(5519271895092943588)
XLA Ops:
  5.4 4.1 %collective-permute-start = (bf16[128,1024]{1,0:T(8,128)(2,1)S(1)}, bf16[128,1024]{1,0:T(8,128)(2,1)}, u32[]{:S(2)}, u32[]{:S(2)}) collective-permute-start(bf16[128,1024]{1,0:T(8,128)(2,1)S(1)} %convolution_convert_fusion.7), channel_id=1, source_target_pairs={{0,2},{1,3},{2,0},{3,1},{4,6},{5,7},{6,4},{7,5},{8,10},{9,11},{10,... | collective-permute-start | bytes 786440 | tf_op jit(solution)/shard_map/ppermute | solution.py:26
  32.5 6.0 %collective-permute-start.8 = (bf16[128,1024]{1,0:T(8,128)(2,1)S(1)}, bf16[128,1024]{1,0:T(8,128)(2,1)S(1)}, u32[]{:S(2)}, u32[]{:S(2)}) collective-permute-start(bf16[128,1024]{1,0:T(8,128)(2,1)S(1)} %copy-done.19), channel_id=1, source_target_pairs={{0,2},{1,3},{2,0},{3,1},{4,6},{5,7},{6,4},{7,5},{8,10},{9,11},{10,... | collective-permute-start | bytes 786440 | tf_op jit(solution)/shard_map/ppermute | solution.py:26
  40.5 5.6 %collective-permute-done.5 = bf16[4,80,1024]{2,1,0:T(8,128)(2,1)S(1)} collective-permute-done((bf16[4,80,1024]{2,1,0:T(8,128)(2,1)S(1)}, bf16[4,80,1024]{2,1,0:T(8,128)(2,1)S(1)}, u32[]{:S(2)}, u32[]{:S(2)}) %collective-permute-start.5) | collective-permute-done | bytes 655392 | tf_op jit(solution)/shard_map/ppermute | solution.py:26
  48.1 7.5 %collective-permute-start.6 = (bf16[2,80,1024]{2,1,0:T(8,128)(2,1)S(1)}, bf16[2,80,1024]{2,1,0:T(8,128)(2,1)S(1)}, u32[]{:S(2)}, u32[]{:S(2)}) collective-permute-start(bf16[2,80,1024]{2,1,0:T(8,128)(2,1)S(1)} %bitcast.207), channel_id=1, source_target_pairs={{0,1},{4,5},{8,9},{12,13},{16,17},{20,21},{24,25},{28,29}} | collective-permute-start | bytes 983048 | tf_op jit(solution)/shard_map/ppermute | solution.py:26
  57.1 5.1 %collective-permute-done.6 = bf16[2,80,1024]{2,1,0:T(8,128)(2,1)S(1)} collective-permute-done((bf16[2,80,1024]{2,1,0:T(8,128)(2,1)S(1)}, bf16[2,80,1024]{2,1,0:T(8,128)(2,1)S(1)}, u32[]{:S(2)}, u32[]{:S(2)}) %collective-permute-start.6) | collective-permute-done | bytes 327712 | tf_op jit(solution)/shard_map/ppermute | solution.py:26
  62.4 4.4 %collective-permute-start.11 = (bf16[2,80,1024]{2,1,0:T(8,128)(2,1)S(1)}, bf16[2,80,1024]{2,1,0:T(8,128)(2,1)S(1)}, u32[]{:S(2)}, u32[]{:S(2)}) collective-permute-start(bf16[2,80,1024]{2,1,0:T(8,128)(2,1)S(1)} %get-tuple-element.131), channel_id=1, source_target_pairs={{0,1},{1,2},{4,5},{5,6},{8,9},{9,10},{12,13},{13,14},{16,17},{17,1... | collective-permute-start | bytes 983048 | tf_op jit(solution)/shard_map/ppermute | solution.py:26
  72.6 8.5 %collective-permute-start.13 = (bf16[2,80,1024]{2,1,0:T(8,128)(2,1)S(1)}, bf16[2,80,1024]{2,1,0:T(8,128)(2,1)S(1)}, u32[]{:S(2)}, u32[]{:S(2)}) collective-permute-start(bf16[2,80,1024]{2,1,0:T(8,128)(2,1)S(1)} %add_convert_fusion.3), channel_id=1, source_target_pairs={{0,1},{1,2},{2,3},{4,5},{5,6},{6,7},{8,9},{9,10},{10,11},{12,13},{... | collective-permute-start | bytes 983048 | tf_op jit(solution)/shard_map/ppermute | solution.py:26
  82.8 2.9 %collective-permute-done.13 = bf16[2,80,1024]{2,1,0:T(8,128)(2,1)S(1)} collective-permute-done((bf16[2,80,1024]{2,1,0:T(8,128)(2,1)S(1)}, bf16[2,80,1024]{2,1,0:T(8,128)(2,1)S(1)}, u32[]{:S(2)}, u32[]{:S(2)}) %collective-permute-start.13) | collective-permute-done | bytes 327712 | tf_op jit(solution)/shard_map/ppermute | solution.py:26
  85.7 5.1 %collective-permute-done.14 = bf16[2,80,1024]{2,1,0:T(8,128)(2,1)S(1)} collective-permute-done((bf16[2,80,1024]{2,1,0:T(8,128)(2,1)S(1)}, bf16[2,80,1024]{2,1,0:T(8,128)(2,1)S(1)}, u32[]{:S(2)}, u32[]{:S(2)}) %collective-permute-start.14) | collective-permute-done | bytes 327712 | tf_op jit(solution)/shard_map/ppermute | solution.py:26
  91.3 4.5 %collective-permute-start.17 = (bf16[2,80,2048]{2,1,0:T(8,128)(2,1)S(1)}, bf16[2,80,2048]{2,1,0:T(8,128)(2,1)}, u32[]{:S(2)}, u32[]{:S(2)}) collective-permute-start(bf16[2,80,2048]{2,1,0:T(8,128)(2,1)S(1)} %pad_maximum_fusion.6), channel_id=1, source_target_pairs={{0,1},{1,2},{2,3},{4,5},{5,6},{6,7},{8,9},{9,10},{10,11},{12,13},{... | collective-permute-start | bytes 1966088 | tf_op jit(solution)/shard_map/ppermute | solution.py:26
  99.5 3.1 %fusion.4 = bf16[640,2048]{1,0:T(8,128)(2,1)S(1)} fusion(bf16[640,1024]{1,0:T(8,128)(2,1)S(1)} %bitcast.204, bf16[1,1,1024,2048]{3,2,1,0:T(8,128)(2,1)S(1)} %copy-done.21), kind=kOutput, calls=%fused_computation.4 | convolution fusion | flops 2685665280 | bytes 8126464 | tf_op jit(solution)/shard_map/dot_general | solution.py:248
  102.7 6.9 %collective-permute-done.20 = s32[128]{0:T(128)S(1)} collective-permute-done((s32[128]{0:T(128)S(1)}, s32[128]{0:T(128)S(1)}, u32[]{:S(2)}, u32[]{:S(2)}) %collective-permute-start.20) | collective-permute-done | bytes 544 | tf_op jit(solution)/shard_map/ppermute | solution.py:26
  109.6 3.5 %collective-permute-done.18 = bf16[2,80,2048]{2,1,0:T(8,128)(2,1)} collective-permute-done((bf16[2,80,2048]{2,1,0:T(8,128)(2,1)S(1)}, bf16[2,80,2048]{2,1,0:T(8,128)(2,1)}, u32[]{:S(2)}, u32[]{:S(2)}) %collective-permute-start.18) | collective-permute-done | bytes 655392 | tf_op jit(solution)/shard_map/ppermute | solution.py:26
  114.3 3.4 %collective-permute-start.22 = (bf16[2,80,2048]{2,1,0:T(8,128)(2,1)S(1)}, bf16[2,80,2048]{2,1,0:T(8,128)(2,1)S(1)}, u32[]{:S(2)}, u32[]{:S(2)}) collective-permute-start(bf16[2,80,2048]{2,1,0:T(8,128)(2,1)S(1)} %bitcast.198), channel_id=1, source_target_pairs={{0,1},{4,5},{8,9},{12,13},{16,17},{20,21},{24,25},{28,29}} | collective-permute-start | bytes 1966088 | tf_op jit(solution)/shard_map/ppermute | solution.py:26
  121.2 9.9 %collective-permute-done.22 = bf16[2,80,2048]{2,1,0:T(8,128)(2,1)S(1)} collective-permute-done((bf16[2,80,2048]{2,1,0:T(8,128)(2,1)S(1)}, bf16[2,80,2048]{2,1,0:T(8,128)(2,1)S(1)}, u32[]{:S(2)}, u32[]{:S(2)}) %collective-permute-start.22) | collective-permute-done | bytes 655392 | tf_op jit(solution)/shard_map/ppermute | solution.py:26
  132.6 5.2 %collective-permute-start.24 = (bf16[2,80,2048]{2,1,0:T(8,128)(2,1)}, bf16[2,80,2048]{2,1,0:T(8,128)(2,1)}, u32[]{:S(2)}, u32[]{:S(2)}) collective-permute-start(bf16[2,80,2048]{2,1,0:T(8,128)(2,1)} %get-tuple-element.129), channel_id=1, source_target_pairs={{0,1},{1,2},{4,5},{5,6},{8,9},{9,10},{12,13},{13,14},{16,17},{17,1... | collective-permute-start | bytes 1966088 | tf_op jit(solution)/shard_map/ppermute | solution.py:26
  142.7 7.3 %collective-permute-done.24 = bf16[2,80,2048]{2,1,0:T(8,128)(2,1)} collective-permute-done((bf16[2,80,2048]{2,1,0:T(8,128)(2,1)}, bf16[2,80,2048]{2,1,0:T(8,128)(2,1)}, u32[]{:S(2)}, u32[]{:S(2)}) %collective-permute-start.24) | collective-permute-done | bytes 655392 | tf_op jit(solution)/shard_map/ppermute | solution.py:26
  152.1 8.7 %collective-permute-start.26 = (bf16[2,80,2048]{2,1,0:T(8,128)(2,1)}, bf16[2,80,2048]{2,1,0:T(8,128)(2,1)}, u32[]{:S(2)}, u32[]{:S(2)}) collective-permute-start(bf16[2,80,2048]{2,1,0:T(8,128)(2,1)} %add_convert_fusion.1), channel_id=1, source_target_pairs={{0,1},{1,2},{2,3},{4,5},{5,6},{6,7},{8,9},{9,10},{10,11},{12,13},{... | collective-permute-start | bytes 1966088 | tf_op jit(solution)/shard_map/ppermute | solution.py:26
  168.0 2.9 %fusion.11 = bf16[640,1024]{1,0:T(8,128)(2,1)S(1)} fusion(bf16[640,2048]{1,0:T(8,128)(2,1)S(1)} %bitcast.196, bf16[1,1,1024,2048]{3,2,1,0:T(8,128)(2,1)S(1)} %copy-done.22), kind=kOutput, calls=%fused_computation.14 | convolution fusion | flops 2685009920 | bytes 8126464 | tf_op jit(solution)/shard_map/dot_general | solution.py:51
  177.0 2.3 collective-permute-done.27
  179.3 8.0 %collective-permute-done.32 = bf16[4,80,1024]{2,1,0:T(8,128)(2,1)} collective-permute-done((bf16[4,80,1024]{2,1,0:T(8,128)(2,1)}, bf16[4,80,1024]{2,1,0:T(8,128)(2,1)}, u32[]{:S(2)}, u32[]{:S(2)}) %collective-permute-start.32) | collective-permute-done | bytes 655392 | tf_op jit(solution)/shard_map/ppermute | solution.py:26
  191.5 2.8 %collective-permute-start.34 = (bf16[2,80,1024]{2,1,0:T(8,128)(2,1)S(1)}, bf16[2,80,1024]{2,1,0:T(8,128)(2,1)S(1)}, u32[]{:S(2)}, u32[]{:S(2)}) collective-permute-start(bf16[2,80,1024]{2,1,0:T(8,128)(2,1)S(1)} %fusion.35), channel_id=1, source_target_pairs={{0,2},{1,3},{2,0},{3,1},{4,6},{5,7},{6,4},{7,5},{8,10},{9,11},{10,... | collective-permute-start | bytes 983048 | tf_op jit(solution)/shard_map/ppermute | solution.py:26
  195.8 3.8 %collective-permute-done.33 = bf16[2,80,1024]{2,1,0:T(8,128)(2,1)S(1)} collective-permute-done((bf16[2,80,1024]{2,1,0:T(8,128)(2,1)S(1)}, bf16[2,80,1024]{2,1,0:T(8,128)(2,1)S(1)}, u32[]{:S(2)}, u32[]{:S(2)}) %collective-permute-start.33) | collective-permute-done | bytes 327712 | tf_op jit(solution)/shard_map/ppermute | solution.py:26
  199.6 19.6 %collective-permute-done.34 = bf16[2,80,1024]{2,1,0:T(8,128)(2,1)S(1)} collective-permute-done((bf16[2,80,1024]{2,1,0:T(8,128)(2,1)S(1)}, bf16[2,80,1024]{2,1,0:T(8,128)(2,1)S(1)}, u32[]{:S(2)}, u32[]{:S(2)}) %collective-permute-start.34) | collective-permute-done | bytes 327712 | tf_op jit(solution)/shard_map/ppermute | solution.py:26
  223.6 4.5 %collective-permute-start.43 = (bf16[128,1024]{1,0:T(8,128)(2,1)S(1)}, bf16[128,1024]{1,0:T(8,128)(2,1)S(1)}, u32[]{:S(2)}, u32[]{:S(2)}) collective-permute-start(bf16[128,1024]{1,0:T(8,128)(2,1)S(1)} %get-tuple-element.123), channel_id=1, source_target_pairs={{0,27},{1,24},{2,25},{3,26},{4,31},{5,28},{6,29},{7,30},{8,3},{9,0... | collective-permute-start | bytes 786440 | tf_op jit(solution)/shard_map/ppermute | solution.py:26
  229.1 5.4 %collective-permute-done.36 = bf16[4,80,1024]{2,1,0:T(8,128)(2,1)S(1)} collective-permute-done((bf16[4,80,1024]{2,1,0:T(8,128)(2,1)S(1)}, bf16[4,80,1024]{2,1,0:T(8,128)(2,1)S(1)}, u32[]{:S(2)}, u32[]{:S(2)}) %collective-permute-start.36) | collective-permute-done | bytes 655392 | tf_op jit(solution)/shard_map/ppermute | solution.py:26
  235.7 2.7 %collective-permute-start.37 = (bf16[128,1024]{1,0:T(8,128)(2,1)}, bf16[128,1024]{1,0:T(8,128)(2,1)}, u32[]{:S(2)}, u32[]{:S(2)}) collective-permute-start(bf16[128,1024]{1,0:T(8,128)(2,1)} %get-tuple-element.115), channel_id=1, source_target_pairs={{0,10},{1,11},{2,8},{3,9},{4,14},{5,15},{6,12},{7,13},{8,18},{9,19... | collective-permute-start | bytes 786440 | tf_op jit(solution)/shard_map/ppermute | solution.py:26
  238.4 4.4 %collective-permute-done.41.refs_0_ = bf16[128,1024]{1,0:T(8,128)(2,1)S(1)} collective-permute-done((bf16[128,1024]{1,0:T(8,128)(2,1)S(1)}, bf16[128,1024]{1,0:T(8,128)(2,1)S(1)}, u32[]{:S(2)}, u32[]{:S(2)}) %collective-permute-start.41) | collective-permute-done | bytes 262176 | tf_op jit(solution)/shard_map/ppermute | solution.py:26
  243.5 3.0 %collective-permute-start.39 = (bf16[128,1024]{1,0:T(8,128)(2,1)}, bf16[128,1024]{1,0:T(8,128)(2,1)}, u32[]{:S(2)}, u32[]{:S(2)}) collective-permute-start(bf16[128,1024]{1,0:T(8,128)(2,1)} %get-tuple-element.117), channel_id=1, source_target_pairs={{0,11},{1,8},{2,9},{3,10},{4,15},{5,12},{6,13},{7,14},{8,19},{9,16... | collective-permute-start | bytes 786440 | tf_op jit(solution)/shard_map/ppermute | solution.py:26
  251.6 2.8 %finish.3 = bf16[1,128,4096]{2,1,0:T(8,128)(2,1)} custom-call(s32[4]{0:T(128)S(1)} %pad_add_fusion.2.at_ref, bf16[128,4096]{1,0:T(8,128)(2,1)S(1)} %copy-done.2, f32[128,1]{1,0:T(8,128)S(1)} %broadcast_in_dim_broadcast_in_dim.3.weight_ref, bf16[128,128]{1,0:T(8,128)(2,1)S(1)} %fusion.60.pick_ref, bf16[128,1024]{1,0:T(8,128)(2,1)S(1)} %collective-permute-done.41.refs_0_, ...), custom_call_target="tpu_custom_call" | custom-call | tf_op jit(solution)/shard_map/finish/pallas_call | solution.py:155
  254.4 10.4 %collective-permute-done.37.refs_0_ = bf16[128,1024]{1,0:T(8,128)(2,1)} collective-permute-done((bf16[128,1024]{1,0:T(8,128)(2,1)}, bf16[128,1024]{1,0:T(8,128)(2,1)}, u32[]{:S(2)}, u32[]{:S(2)}) %collective-permute-start.37) | collective-permute-done | bytes 262176 | tf_op jit(solution)/shard_map/ppermute | solution.py:26
  265.2 3.4 %finish.2 = bf16[1,128,4096]{2,1,0:T(8,128)(2,1)} custom-call(s32[4]{0:T(128)S(1)} %pad_add_fusion.2.at_ref, bf16[128,4096]{1,0:T(8,128)(2,1)S(1)} %collective-permute-done.16.residual_ref, f32[128,1]{1,0:T(8,128)S(1)} %copy.22.weight_ref, bf16[128,128]{1,0:T(8,128)(2,1)S(1)} %fusion.59.pick_ref, bf16[128,1024]{1,0:T(8,128)(2,1)} %collective-permute-done.37.refs_0_, ...), custom_call_target="tpu_custom_call" | custom-call | tf_op jit(solution)/shard_map/finish/pallas_call | solution.py:155
  (185 shorter events, 86.8 us)
Async XLA Ops:
  5.4 24.1 %collective-permute-start = (bf16[128,1024]{1,0:T(8,128)(2,1)S(1)}, bf16[128,1024]{1,0:T(8,128)(2,1)}, u32[]{:S(2)}, u32[]{:S(2)}) collective-permute-start(bf16[128,1024]{1,0:T(8,128)(2,1)S(1)} %convolution_convert_fusion.7), channel_id=1, source_target_pairs={{0,2},{1,3},{2,0},{3,1},{4,6},{5,7},{6,4},{7,5},{8,10},{9,11},{10,... | collective-permute-start | bytes 786440 | tf_op jit(solution)/shard_map/ppermute | solution.py:26
  10.4 19.1 %collective-permute-start.1 = (bf16[128,1024]{1,0:T(8,128)(2,1)}, bf16[128,1024]{1,0:T(8,128)(2,1)}, u32[]{:S(2)}, u32[]{:S(2)}) collective-permute-start(bf16[128,1024]{1,0:T(8,128)(2,1)} %convolution_convert_fusion.6), channel_id=1, source_target_pairs={{0,3},{1,0},{2,1},{3,2},{4,7},{5,4},{6,5},{7,6},{8,11},{9,8},{10,9... | collective-permute-start | bytes 786440 | tf_op jit(solution)/shard_map/ppermute | solution.py:26
  12.7 16.8 %collective-permute-start.2 = (bf16[128,1024]{1,0:T(8,128)(2,1)}, bf16[128,1024]{1,0:T(8,128)(2,1)}, u32[]{:S(2)}, u32[]{:S(2)}) collective-permute-start(bf16[128,1024]{1,0:T(8,128)(2,1)} %convolution_convert_fusion.5), channel_id=1, source_target_pairs={{0,1},{1,2},{2,3},{3,0},{4,5},{5,6},{6,7},{7,4},{8,9},{9,10},{10,1... | collective-permute-start | bytes 786440 | tf_op jit(solution)/shard_map/ppermute | solution.py:26
  14.8 14.7 %collective-permute-start.3 = (bf16[80,2048]{1,0:T(8,128)(2,1)S(1)}, bf16[80,2048]{1,0:T(8,128)(2,1)S(1)}, u32[]{:S(2)}, u32[]{:S(2)}) collective-permute-start(bf16[80,2048]{1,0:T(8,128)(2,1)S(1)} %broadcast_select_fusion.5), channel_id=1, source_target_pairs={{0,4},{1,5},{2,6},{3,7},{4,0},{5,1},{6,2},{7,3},{8,12},{9,13},{10,... | collective-permute-start | bytes 983048 | tf_op jit(solution)/shard_map/ppermute | solution.py:26
  30.9 15.1 %collective-permute-start.5 = (bf16[4,80,1024]{2,1,0:T(8,128)(2,1)S(1)}, bf16[4,80,1024]{2,1,0:T(8,128)(2,1)S(1)}, u32[]{:S(2)}, u32[]{:S(2)}) collective-permute-start(bf16[4,80,1024]{2,1,0:T(8,128)(2,1)S(1)} %broadcast_select_fusion.2), channel_id=1, source_target_pairs={{0,4},{1,5},{2,6},{3,7},{4,0},{5,1},{6,2},{7,3},{8,12},{9,13},{10,... | collective-permute-start | bytes 1966088 | tf_op jit(solution)/shard_map/ppermute | solution.py:26
  32.5 23.9 %collective-permute-start.8 = (bf16[128,1024]{1,0:T(8,128)(2,1)S(1)}, bf16[128,1024]{1,0:T(8,128)(2,1)S(1)}, u32[]{:S(2)}, u32[]{:S(2)}) collective-permute-start(bf16[128,1024]{1,0:T(8,128)(2,1)S(1)} %copy-done.19), channel_id=1, source_target_pairs={{0,2},{1,3},{2,0},{3,1},{4,6},{5,7},{6,4},{7,5},{8,10},{9,11},{10,... | collective-permute-start | bytes 786440 | tf_op jit(solution)/shard_map/ppermute | solution.py:26
  38.4 18.6 %collective-permute-start.9 = (bf16[128,1024]{1,0:T(8,128)(2,1)S(1)}, bf16[128,1024]{1,0:T(8,128)(2,1)S(1)}, u32[]{:S(2)}, u32[]{:S(2)}) collective-permute-start(bf16[128,1024]{1,0:T(8,128)(2,1)S(1)} %copy-done.18), channel_id=1, source_target_pairs={{0,3},{1,0},{2,1},{3,2},{4,7},{5,4},{6,5},{7,6},{8,11},{9,8},{10,9... | collective-permute-start | bytes 786440 | tf_op jit(solution)/shard_map/ppermute | solution.py:26
  38.9 18.2 %collective-permute-start.10 = (bf16[128,1024]{1,0:T(8,128)(2,1)S(1)}, bf16[128,1024]{1,0:T(8,128)(2,1)S(1)}, u32[]{:S(2)}, u32[]{:S(2)}) collective-permute-start(bf16[128,1024]{1,0:T(8,128)(2,1)S(1)} %convolution_convert_fusion.1), channel_id=1, source_target_pairs={{0,1},{1,2},{2,3},{3,0},{4,5},{5,6},{6,7},{7,4},{8,9},{9,10},{10,1... | collective-permute-start | bytes 786440 | tf_op jit(solution)/shard_map/ppermute | solution.py:26
  68.9 21.9 %collective-permute-start.16 = (bf16[128,4096]{1,0:T(8,128)(2,1)S(1)}, bf16[128,4096]{1,0:T(8,128)(2,1)S(1)}, u32[]{:S(2)}, u32[]{:S(2)}) collective-permute-start(bf16[128,4096]{1,0:T(8,128)(2,1)S(1)} %bitcast.217), channel_id=1, source_target_pairs={{0,8},{1,9},{2,10},{3,11},{4,12},{5,13},{6,14},{7,15},{8,16},{9,17... | collective-permute-start | bytes 3145736 | tf_op jit(solution)/shard_map/ppermute | solution.py:26
  70.2 20.6 %collective-permute-start.15 = (bf16[4,80,1024]{2,1,0:T(8,128)(2,1)S(1)}, bf16[4,80,1024]{2,1,0:T(8,128)(2,1)S(1)}, u32[]{:S(2)}, u32[]{:S(2)}) collective-permute-start(bf16[4,80,1024]{2,1,0:T(8,128)(2,1)S(1)} %broadcast_select_fusion.1), channel_id=1, source_target_pairs={{0,4},{1,5},{2,6},{3,7},{4,0},{5,1},{6,2},{7,3},{8,12},{9,13},{10,... | collective-permute-start | bytes 1966088 | tf_op jit(solution)/shard_map/ppermute | solution.py:26
  91.3 18.3 %collective-permute-start.17 = (bf16[2,80,2048]{2,1,0:T(8,128)(2,1)S(1)}, bf16[2,80,2048]{2,1,0:T(8,128)(2,1)}, u32[]{:S(2)}, u32[]{:S(2)}) collective-permute-start(bf16[2,80,2048]{2,1,0:T(8,128)(2,1)S(1)} %pad_maximum_fusion.6), channel_id=1, source_target_pairs={{0,1},{1,2},{2,3},{4,5},{5,6},{6,7},{8,9},{9,10},{10,11},{12,13},{... | collective-permute-start | bytes 1966088 | tf_op jit(solution)/shard_map/ppermute | solution.py:26
  95.9 17.2 %collective-permute-start.18 = (bf16[2,80,2048]{2,1,0:T(8,128)(2,1)S(1)}, bf16[2,80,2048]{2,1,0:T(8,128)(2,1)}, u32[]{:S(2)}, u32[]{:S(2)}) collective-permute-start(bf16[2,80,2048]{2,1,0:T(8,128)(2,1)S(1)} %pad_maximum_fusion.6), channel_id=1, source_target_pairs={{1,0},{2,1},{3,2},{5,4},{6,5},{7,6},{9,8},{10,9},{11,10},{13,12},{... | collective-permute-start | bytes 1966088 | tf_op jit(solution)/shard_map/ppermute | solution.py:26
  97.2 15.9 %collective-permute-start.19 = (bf16[128,4096]{1,0:T(8,128)(2,1)S(1)}, bf16[128,4096]{1,0:T(8,128)(2,1)S(1)}, u32[]{:S(2)}, u32[]{:S(2)}) collective-permute-start(bf16[128,4096]{1,0:T(8,128)(2,1)S(1)} %bitcast.216), channel_id=1, source_target_pairs={{0,24},{1,25},{2,26},{3,27},{4,28},{5,29},{6,30},{7,31},{8,0},{9,1... | collective-permute-start | bytes 3145736 | tf_op jit(solution)/shard_map/ppermute | solution.py:26
  114.3 16.9 %collective-permute-start.22 = (bf16[2,80,2048]{2,1,0:T(8,128)(2,1)S(1)}, bf16[2,80,2048]{2,1,0:T(8,128)(2,1)S(1)}, u32[]{:S(2)}, u32[]{:S(2)}) collective-permute-start(bf16[2,80,2048]{2,1,0:T(8,128)(2,1)S(1)} %bitcast.198), channel_id=1, source_target_pairs={{0,1},{4,5},{8,9},{12,13},{16,17},{20,21},{24,25},{28,29}} | collective-permute-start | bytes 1966088 | tf_op jit(solution)/shard_map/ppermute | solution.py:26
  118.4 20.9 %collective-permute-start.28 = (bf16[2,80,2048]{2,1,0:T(8,128)(2,1)}, bf16[2,80,2048]{2,1,0:T(8,128)(2,1)}, u32[]{:S(2)}, u32[]{:S(2)}) collective-permute-start(bf16[2,80,2048]{2,1,0:T(8,128)(2,1)} %collective-permute-done.17), channel_id=1, source_target_pairs={{1,2},{2,3},{5,6},{6,7},{9,10},{10,11},{13,14},{14,15},{17,18},{18... | collective-permute-start | bytes 1966088 | tf_op jit(solution)/shard_map/ppermute | solution.py:26
  120.0 19.4 %collective-permute-start.29 = (bf16[2,80,2048]{2,1,0:T(8,128)(2,1)}, bf16[2,80,2048]{2,1,0:T(8,128)(2,1)}, u32[]{:S(2)}, u32[]{:S(2)}) collective-permute-start(bf16[2,80,2048]{2,1,0:T(8,128)(2,1)} %collective-permute-done.18), channel_id=1, source_target_pairs={{1,0},{2,1},{5,4},{6,5},{9,8},{10,9},{13,12},{14,13},{17,16},{18,1... | collective-permute-start | bytes 1966088 | tf_op jit(solution)/shard_map/ppermute | solution.py:26
  132.6 17.3 %collective-permute-start.24 = (bf16[2,80,2048]{2,1,0:T(8,128)(2,1)}, bf16[2,80,2048]{2,1,0:T(8,128)(2,1)}, u32[]{:S(2)}, u32[]{:S(2)}) collective-permute-start(bf16[2,80,2048]{2,1,0:T(8,128)(2,1)} %get-tuple-element.129), channel_id=1, source_target_pairs={{0,1},{1,2},{4,5},{5,6},{8,9},{9,10},{12,13},{13,14},{16,17},{17,1... | collective-permute-start | bytes 1966088 | tf_op jit(solution)/shard_map/ppermute | solution.py:26
  139.4 25.1 %collective-permute-start.31 = (bf16[2,80,2048]{2,1,0:T(8,128)(2,1)}, bf16[2,80,2048]{2,1,0:T(8,128)(2,1)S(1)}, u32[]{:S(2)}, u32[]{:S(2)}) collective-permute-start(bf16[2,80,2048]{2,1,0:T(8,128)(2,1)} %collective-permute-done.29), channel_id=1, source_target_pairs={{1,0},{5,4},{9,8},{13,12},{17,16},{21,20},{25,24},{29,28}} | collective-permute-start | bytes 1966088 | tf_op jit(solution)/shard_map/ppermute | solution.py:26
  140.8 23.8 %collective-permute-start.30 = (bf16[2,80,2048]{2,1,0:T(8,128)(2,1)}, bf16[2,80,2048]{2,1,0:T(8,128)(2,1)S(1)}, u32[]{:S(2)}, u32[]{:S(2)}) collective-permute-start(bf16[2,80,2048]{2,1,0:T(8,128)(2,1)} %collective-permute-done.28), channel_id=1, source_target_pairs={{2,3},{6,7},{10,11},{14,15},{18,19},{22,23},{26,27},{30,31}} | collective-permute-start | bytes 1966088 | tf_op jit(solution)/shard_map/ppermute | solution.py:26
  152.1 24.9 %collective-permute-start.26 = (bf16[2,80,2048]{2,1,0:T(8,128)(2,1)}, bf16[2,80,2048]{2,1,0:T(8,128)(2,1)}, u32[]{:S(2)}, u32[]{:S(2)}) collective-permute-start(bf16[2,80,2048]{2,1,0:T(8,128)(2,1)} %add_convert_fusion.1), channel_id=1, source_target_pairs={{0,1},{1,2},{2,3},{4,5},{5,6},{6,7},{8,9},{9,10},{10,11},{12,13},{... | collective-permute-start | bytes 1966088 | tf_op jit(solution)/shard_map/ppermute | solution.py:26
  163.0 16.3 %collective-permute-start.27 = (bf16[2,80,2048]{2,1,0:T(8,128)(2,1)}, bf16[2,80,2048]{2,1,0:T(8,128)(2,1)}, u32[]{:S(2)}, u32[]{:S(2)}) collective-permute-start(bf16[2,80,2048]{2,1,0:T(8,128)(2,1)} %add_convert_fusion), channel_id=1, source_target_pairs={{1,0},{2,1},{3,2},{5,4},{6,5},{7,6},{9,8},{10,9},{11,10},{13,12},{... | collective-permute-start | bytes 1966088 | tf_op jit(solution)/shard_map/ppermute | solution.py:26
  172.9 14.4 %collective-permute-start.32 = (bf16[4,80,1024]{2,1,0:T(8,128)(2,1)}, bf16[4,80,1024]{2,1,0:T(8,128)(2,1)}, u32[]{:S(2)}, u32[]{:S(2)}) collective-permute-start(bf16[4,80,1024]{2,1,0:T(8,128)(2,1)} %dynamic-slice_bitcast_fusion.1), channel_id=1, source_target_pairs={{0,4},{1,5},{2,6},{3,7},{4,0},{5,1},{6,2},{7,3},{8,12},{9,13},{10,... | collective-permute-start | bytes 1966088 | tf_op jit(solution)/shard_map/ppermute | solution.py:26
  191.5 27.8 %collective-permute-start.34 = (bf16[2,80,1024]{2,1,0:T(8,128)(2,1)S(1)}, bf16[2,80,1024]{2,1,0:T(8,128)(2,1)S(1)}, u32[]{:S(2)}, u32[]{:S(2)}) collective-permute-start(bf16[2,80,1024]{2,1,0:T(8,128)(2,1)S(1)} %fusion.35), channel_id=1, source_target_pairs={{0,2},{1,3},{2,0},{3,1},{4,6},{5,7},{6,4},{7,5},{8,10},{9,11},{10,... | collective-permute-start | bytes 983048 | tf_op jit(solution)/shard_map/ppermute | solution.py:26
  194.3 24.9 %collective-permute-start.35 = (bf16[2,80,1024]{2,1,0:T(8,128)(2,1)S(1)}, bf16[2,80,1024]{2,1,0:T(8,128)(2,1)S(1)}, u32[]{:S(2)}, u32[]{:S(2)}) collective-permute-start(bf16[2,80,1024]{2,1,0:T(8,128)(2,1)S(1)} %fusion.35), channel_id=1, source_target_pairs={{0,1},{1,2},{2,3},{3,0},{4,5},{5,6},{6,7},{7,4},{8,9},{9,10},{10,1... | collective-permute-start | bytes 983048 | tf_op jit(solution)/shard_map/ppermute | solution.py:26
  223.6 19.1 %collective-permute-start.41 = (bf16[128,1024]{1,0:T(8,128)(2,1)S(1)}, bf16[128,1024]{1,0:T(8,128)(2,1)S(1)}, u32[]{:S(2)}, u32[]{:S(2)}) collective-permute-start(bf16[128,1024]{1,0:T(8,128)(2,1)S(1)} %get-tuple-element.125), channel_id=1, source_target_pairs={{0,26},{1,27},{2,24},{3,25},{4,30},{5,31},{6,28},{7,29},{8,2},{9,3... | collective-permute-start | bytes 786440 | tf_op jit(solution)/shard_map/ppermute | solution.py:26
  223.6 19.1 %collective-permute-start.42 = (bf16[128,1024]{1,0:T(8,128)(2,1)S(1)}, bf16[128,1024]{1,0:T(8,128)(2,1)S(1)}, u32[]{:S(2)}, u32[]{:S(2)}) collective-permute-start(bf16[128,1024]{1,0:T(8,128)(2,1)S(1)} %get-tuple-element.124), channel_id=1, source_target_pairs={{0,25},{1,26},{2,27},{3,24},{4,29},{5,30},{6,31},{7,28},{8,1},{9,2... | collective-permute-start | bytes 786440 | tf_op jit(solution)/shard_map/ppermute | solution.py:26
  223.6 22.8 %collective-permute-start.43 = (bf16[128,1024]{1,0:T(8,128)(2,1)S(1)}, bf16[128,1024]{1,0:T(8,128)(2,1)S(1)}, u32[]{:S(2)}, u32[]{:S(2)}) collective-permute-start(bf16[128,1024]{1,0:T(8,128)(2,1)S(1)} %get-tuple-element.123), channel_id=1, source_target_pairs={{0,27},{1,24},{2,25},{3,26},{4,31},{5,28},{6,29},{7,30},{8,3},{9,0... | collective-permute-start | bytes 786440 | tf_op jit(solution)/shard_map/ppermute | solution.py:26
  228.2 20.3 %collective-permute-start.44 = (bf16[128,1024]{1,0:T(8,128)(2,1)}, bf16[128,1024]{1,0:T(8,128)(2,1)}, u32[]{:S(2)}, u32[]{:S(2)}) collective-permute-start(bf16[128,1024]{1,0:T(8,128)(2,1)} %get-tuple-element.122), channel_id=1, source_target_pairs={{0,24},{1,25},{2,26},{3,27},{4,28},{5,29},{6,30},{7,31},{8,0},{9,1... | collective-permute-start | bytes 786440 | tf_op jit(solution)/shard_map/ppermute | solution.py:26
  235.7 29.1 %collective-permute-start.37 = (bf16[128,1024]{1,0:T(8,128)(2,1)}, bf16[128,1024]{1,0:T(8,128)(2,1)}, u32[]{:S(2)}, u32[]{:S(2)}) collective-permute-start(bf16[128,1024]{1,0:T(8,128)(2,1)} %get-tuple-element.115), channel_id=1, source_target_pairs={{0,10},{1,11},{2,8},{3,9},{4,14},{5,15},{6,12},{7,13},{8,18},{9,19... | collective-permute-start | bytes 786440 | tf_op jit(solution)/shard_map/ppermute | solution.py:26
  242.7 22.1 %collective-permute-start.38 = (bf16[128,1024]{1,0:T(8,128)(2,1)}, bf16[128,1024]{1,0:T(8,128)(2,1)}, u32[]{:S(2)}, u32[]{:S(2)}) collective-permute-start(bf16[128,1024]{1,0:T(8,128)(2,1)} %get-tuple-element.116), channel_id=1, source_target_pairs={{0,9},{1,10},{2,11},{3,8},{4,13},{5,14},{6,15},{7,12},{8,17},{9,18... | collective-permute-start | bytes 786440 | tf_op jit(solution)/shard_map/ppermute | solution.py:26
  243.5 21.7 %collective-permute-start.39 = (bf16[128,1024]{1,0:T(8,128)(2,1)}, bf16[128,1024]{1,0:T(8,128)(2,1)}, u32[]{:S(2)}, u32[]{:S(2)}) collective-permute-start(bf16[128,1024]{1,0:T(8,128)(2,1)} %get-tuple-element.117), channel_id=1, source_target_pairs={{0,11},{1,8},{2,9},{3,10},{4,15},{5,12},{6,13},{7,14},{8,19},{9,16... | collective-permute-start | bytes 786440 | tf_op jit(solution)/shard_map/ppermute | solution.py:26
  247.1 18.0 %collective-permute-start.40 = (bf16[128,1024]{1,0:T(8,128)(2,1)}, bf16[128,1024]{1,0:T(8,128)(2,1)}, u32[]{:S(2)}, u32[]{:S(2)}) collective-permute-start(bf16[128,1024]{1,0:T(8,128)(2,1)} %get-tuple-element.114), channel_id=1, source_target_pairs={{0,8},{1,9},{2,10},{3,11},{4,12},{5,13},{6,14},{7,15},{8,16},{9,17... | collective-permute-start | bytes 786440 | tf_op jit(solution)/shard_map/ppermute | solution.py:26
  (39 other events, 315.4 us)
where the time goes:
time: 273 us; the launch traced here: 269 us
  waiting for transfers between devices  102 us (37%)
  starting transfers between devices  94.6 us (35%)
  other arithmetic  25.9 us (9%)
  matrix products  21.9 us (8%)
  local copies, waits for them, and re-layouts  13.6 us (5%)
  Pallas kernels  6.14 us (2%)
  between operations  4.13 us (2%)
    ppermute x45, waiting for transfers between devices, move(): return lax.ppermute(value, AXES, pairs)  102 us
    ppermute x45, starting transfers between devices, move(): return lax.ppermute(value, AXES, pairs)  94.6 us
    unnamed x52, local copies, waits for them, and re-layouts  10 us
    dot_general x8, matrix products, cut(): jnp.dot(placer, block, preferred_element_type=F32).astype(BF16)  9.42 us
    convert_element_type x6, other arithmetic, sums(): right, left = (right.astype(BF16), left.astype(BF16))  6.16 us
    pallas_call x2, Pallas kernels, finish(): pl.pallas_call(finish_kernel, out_shape=jax.ShapeDtypeStruct((1, tokens,...  6.14 us
  transfers between devices with their start and end apart: 45, of which 18 were waited for; matrix products, arithmetic and copies ran while one was open for 15% of the time, Pallas kernels for 1%

commit v1 on v0

--- a/solution.py
+++ b/solution.py
@@ -180,7 +180,7 @@
 
     act, grad = act_fwd[0], grad_bwd[0]
     route_a, route_b = routes_fwd[0, :, 0], routes_bwd[0, :, 0]
-    sort_a, sort_b = sorter(route_a), sorter(route_b)
+    sort_a = sorter(route_a)
     zeros = tokens_here - jnp.stack([jnp.sum(route_a), jnp.sum(route_b)]).astype(F32)
 
     def in_rows(cuts, got):
@@ -199,16 +199,18 @@
         return operands(pieces), send(pieces)
 
     dy = (weight_bwd[0][:, None] * grad.astype(F32)).astype(BF16)
+    sort_b = sorter(route_b)
     cut_b = cut(dy, sort_b, local)
     got_b = [move(cut_b[m], by_local=-m) for m in (2, 1, 3)]
     saved = jnp.dot(sort_b, saved_bwd[0], preferred_element_type=F32).astype(BF16)
     saved_own, saved_other = windows(saved, node, capacity)
-    saved_got = move(saved_other, by_node=1)
-    (zeros_wait,) = after([zeros], saved_other)
-    zeros_got = move(zeros_wait, by_node=1)
+    extra = jnp.broadcast_to(jnp.repeat(zeros, 8)[:, None], (16, saved.shape[1])).astype(BF16)
+    saved_got = move(jnp.concatenate([saved_other, extra], axis=0), by_node=1)
     cut_a = cut(act, sort_a, local)
-    *got_b, saved_got, zeros_got, a0, a1, a2, a3 = join(*got_b, saved_got, zeros_got, *cut_a)
+    *got_b, saved_got, a0, a1, a2, a3 = join(*got_b, saved_got, *cut_a)
     cut_a = [a0, a1, a2, a3]
+    zeros_got = saved_got[capacity::8, 0].astype(F32)
+    saved_got = saved_got[:capacity]
     zeros = by_node(zeros, zeros_got, 0)
     got_a = [move(cut_a[m], by_local=-m) for m in (2, 1, 3)]
     own_b, other_b = in_rows(cut_b, got_b)
@@ -217,16 +219,12 @@
 
     rows_b = by_node(own_b, got_bx, 1).reshape(-1, column)
     part_b = dot_t(rows_b, w_dn).astype(BF16).reshape(shape + (hidden_units,))
-    chain_b = sums(lambda slot: part_b[slot])
-    back_b = send(next(chain_b))
-    *back_b, g0, g1, g2 = join(*back_b, *got_a)
-    own_a, other_a = in_rows(cut_a, [g0, g1, g2])
+    back_b = [move(part_b[m], by_local=m) for m in (2, 1, 3)]
+    both = join(*back_b, *got_a)
+    back_b, got_a = both[:3], both[3:]
+    own_a, other_a = in_rows(cut_a, got_a)
     got_ax = move(other_a, by_node=1)
-    act_next = move(after([act], other_a)[0], by_pp=1)
-    values_b, back_b = turn(chain_b, back_b)
-    values_b, back_b = turn(chain_b, back_b)
-    *back_b, got_ax, act_next = join(*back_b, got_ax, act_next)
-    dh = chain_b.send(back_b)
+    dh = part_b[0].astype(F32) + sum(part.astype(F32) for part in back_b)
     dh = jnp.where(valid(zeros[:, 1], node, tokens_here, capacity)[..., None], dh, 0.0)
     saved_rows = by_node(saved_own, saved_got, 0)
     g = saved_rows[..., :hidden_units].astype(F32)
@@ -238,29 +236,30 @@
 
     chain_b = gathers(grad_gu, local)
     back_b = send(next(chain_b))
-    grad_wait, route_wait, small_wait = after(
-        [grad, route_b, jnp.stack([route_a.astype(F32), weight_fwd[0]])], grad_gu
-    )
-    grad_next = move(grad_wait, by_pp=-1)
+    small_wait, route_wait = after(
+        [jnp.stack([route_a.astype(F32), weight_fwd[0]]), route_b], grad_gu
+    )
+    small_next = move(small_wait, by_pp=1)
     route_b_next = move(route_wait, by_pp=-1)
-    small_next = move(small_wait, by_pp=1)
     rows_a = by_node(own_a, got_ax, 1).reshape(-1, column)
     part_a = jnp.dot(rows_a, w_gu, preferred_element_type=F32).astype(BF16)
-    *back_b, part_a, grad_next, route_b_next, small_next = join(
-        *back_b, part_a, grad_next, route_b_next, small_next
-    )
+    *back_b, part_a, small_next, route_b_next = join(*back_b, part_a, small_next, route_b_next)
     part_a = part_a.reshape(shape + (2 * hidden_units,))
     chain_a = sums(lambda slot: part_a[slot])
     values_b, back_b = turn(chain_b, back_b)
-    back_a = send(next(chain_a))
+    pieces = next(chain_a)
+    back_a = send(pieces)
+    act_next = move(after([act], *operands(pieces))[0], by_pp=1)
+    *back_b, act_next = join(*back_b, act_next)
     values_b, back_b = turn(chain_b, back_b)
+    grad_next = move(join(grad, *values_b)[0], by_pp=-1)
+    *back_b, grad_next = join(*back_b, grad_next)
     values_a, back_a = turn(chain_a, back_a)
     values_a, back_a = turn(chain_a, back_a)
     all_gu = chain_b.send(back_b)
     done_b = dot_t(all_gu.reshape(-1, 2 * hidden_units), w_gu).astype(BF16)
     own_b, other_b = split(done_b.reshape(shape + (column,)))
     got_b = move(other_b, by_node=1)
-    *back_a, got_b = join(*back_a, got_b)
 
     preact = chain_a.send(back_a)
     preact = jnp.where(valid(zeros[:, 0], node, tokens_here, capacity)[..., None], preact, 0.0)

time: 273 us -> 274 us (level)
  starting transfers between devices: 94.6 us -> 104 us
  waiting for transfers between devices: 102 us -> 93.7 us
    ppermute x45 -> x41, starting transfers between devices: 94.6 us -> 104 us  [move(): return lax.ppermute(value, AXES, pairs)]
    ppermute x45 -> x41, waiting for transfers between devices: 102 us -> 93.7 us  [move(): return lax.ppermute(value, AXES, pairs)]
    unnamed x52 -> x42, local copies, waits for them, and re-layouts: 10 us -> 10.9 us
    convert_element_type x6 -> x3, other arithmetic: 6.16 us -> 5.93 us  [sums(): right, left = (right.astype(BF16), left.astype(BF16))]
  transfers between devices with their start and end apart: 45 -> 41, of which waited for: 18 -> 16; matrix products, arithmetic and copies ran while one was open for 15% -> 14% of each run, Pallas kernels for 1% -> 1%
where the time goes in v1:
time: 274 us; the launch traced here: 272 us
  starting transfers between devices  104 us (38%)
  waiting for transfers between devices  93.7 us (34%)
  other arithmetic  27 us (10%)
  matrix products  21.6 us (8%)
  local copies, waits for them, and re-layouts  15.1 us (6%)
  Pallas kernels  6.74 us (2%)
  between operations  3.97 us (1%)
    ppermute x41, starting transfers between devices, move(): return lax.ppermute(value, AXES, pairs)  104 us
    ppermute x41, waiting for transfers between devices, move(): return lax.ppermute(value, AXES, pairs)  93.7 us
    unnamed x42, local copies, waits for them, and re-layouts  10.9 us
    dot_general x8, matrix products, cut(): jnp.dot(placer, block, preferred_element_type=F32).astype(BF16)  9.83 us
    pallas_call x2, Pallas kernels, finish(): pl.pallas_call(finish_kernel, out_shape=jax.ShapeDtypeStruct((1, tokens,...  6.74 us
    convert_element_type x3, other arithmetic, sums(): right, left = (right.astype(BF16), left.astype(BF16))  5.93 us
  transfers between devices with their start and end apart: 41, of which 16 were waited for; matrix products, arithmetic and copies ran while one was open for 14% of the time, Pallas kernels for 1%

profile of v1, /device:TPU:0, one launch (start us, length us, event | category | flops | bytes accessed | tf_op | source)
XLA Modules:
  0.0 272.1 jit_solution(9163491007162149324)
XLA Ops:
  10.9 2.9 %collective-permute-start.3 = (bf16[96,2048]{1,0:T(8,128)(2,1)}, bf16[96,2048]{1,0:T(8,128)(2,1)}, u32[]{:S(2)}, u32[]{:S(2)}) collective-permute-start(bf16[96,2048]{1,0:T(8,128)(2,1)} %pad_maximum_fusion.7), channel_id=1, source_target_pairs={{0,4},{1,5},{2,6},{3,7},{4,0},{5,1},{6,2},{7,3},{8,12},{9,13},{10,... | collective-permute-start | bytes 1179656 | tf_op jit(solution)/shard_map/ppermute | solution.py:26
  16.3 2.6 collective-permute-start
  31.3 6.5 %collective-permute-done = bf16[128,1024]{1,0:T(8,128)(2,1)} collective-permute-done((bf16[128,1024]{1,0:T(8,128)(2,1)}, bf16[128,1024]{1,0:T(8,128)(2,1)}, u32[]{:S(2)}, u32[]{:S(2)}) %collective-permute-start) | collective-permute-done | bytes 262176 | tf_op jit(solution)/shard_map/ppermute | solution.py:26
  41.1 7.1 %collective-permute-start.8 = (bf16[128,1024]{1,0:T(8,128)(2,1)}, bf16[128,1024]{1,0:T(8,128)(2,1)S(1)}, u32[]{:S(2)}, u32[]{:S(2)}) collective-permute-start(bf16[128,1024]{1,0:T(8,128)(2,1)} %convolution_convert_fusion.3), channel_id=1, source_target_pairs={{0,2},{1,3},{2,0},{3,1},{4,6},{5,7},{6,4},{7,5},{8,10},{9,11},{10,... | collective-permute-start | bytes 786440 | tf_op jit(solution)/shard_map/ppermute | solution.py:26
  51.5 3.9 %collective-permute-done.4 = bf16[4,80,1024]{2,1,0:T(8,128)(2,1)} collective-permute-done((bf16[4,80,1024]{2,1,0:T(8,128)(2,1)}, bf16[4,80,1024]{2,1,0:T(8,128)(2,1)}, u32[]{:S(2)}, u32[]{:S(2)}) %collective-permute-start.4) | collective-permute-done | bytes 655392 | tf_op jit(solution)/shard_map/ppermute | solution.py:26
  58.5 4.3 %collective-permute-start.7 = (bf16[2,80,1024]{2,1,0:T(8,128)(2,1)S(1)}, bf16[2,80,1024]{2,1,0:T(8,128)(2,1)S(1)}, u32[]{:S(2)}, u32[]{:S(2)}) collective-permute-start(bf16[2,80,1024]{2,1,0:T(8,128)(2,1)S(1)} %bitcast.211), channel_id=1, source_target_pairs={{0,3},{1,0},{2,1},{3,2},{4,7},{5,4},{6,5},{7,6},{8,11},{9,8},{10,9... | collective-permute-start | bytes 983048 | tf_op jit(solution)/shard_map/ppermute | solution.py:26
  62.8 2.4 collective-permute-start.6
  65.2 3.9 %collective-permute-start.5 = (bf16[2,80,1024]{2,1,0:T(8,128)(2,1)S(1)}, bf16[2,80,1024]{2,1,0:T(8,128)(2,1)S(1)}, u32[]{:S(2)}, u32[]{:S(2)}) collective-permute-start(bf16[2,80,1024]{2,1,0:T(8,128)(2,1)S(1)} %bitcast.209), channel_id=1, source_target_pairs={{0,2},{1,3},{2,0},{3,1},{4,6},{5,7},{6,4},{7,5},{8,10},{9,11},{10,... | collective-permute-start | bytes 983048 | tf_op jit(solution)/shard_map/ppermute | solution.py:26
  70.6 3.9 %collective-permute-done.7 = bf16[2,80,1024]{2,1,0:T(8,128)(2,1)S(1)} collective-permute-done((bf16[2,80,1024]{2,1,0:T(8,128)(2,1)S(1)}, bf16[2,80,1024]{2,1,0:T(8,128)(2,1)S(1)}, u32[]{:S(2)}, u32[]{:S(2)}) %collective-permute-start.7) | collective-permute-done | bytes 327712 | tf_op jit(solution)/shard_map/ppermute | solution.py:26
  74.6 9.7 %collective-permute-done.6 = bf16[2,80,1024]{2,1,0:T(8,128)(2,1)S(1)} collective-permute-done((bf16[2,80,1024]{2,1,0:T(8,128)(2,1)S(1)}, bf16[2,80,1024]{2,1,0:T(8,128)(2,1)S(1)}, u32[]{:S(2)}, u32[]{:S(2)}) %collective-permute-start.6) | collective-permute-done | bytes 327712 | tf_op jit(solution)/shard_map/ppermute | solution.py:26
  84.3 15.3 %collective-permute-done.5 = bf16[2,80,1024]{2,1,0:T(8,128)(2,1)S(1)} collective-permute-done((bf16[2,80,1024]{2,1,0:T(8,128)(2,1)S(1)}, bf16[2,80,1024]{2,1,0:T(8,128)(2,1)S(1)}, u32[]{:S(2)}, u32[]{:S(2)}) %collective-permute-start.5) | collective-permute-done | bytes 327712 | tf_op jit(solution)/shard_map/ppermute | solution.py:26
  104.1 4.6 %collective-permute-start.11 = (bf16[2,80,2048]{2,1,0:T(8,128)(2,1)S(1)}, bf16[2,80,2048]{2,1,0:T(8,128)(2,1)S(1)}, u32[]{:S(2)}, u32[]{:S(2)}) collective-permute-start(bf16[2,80,2048]{2,1,0:T(8,128)(2,1)S(1)} %pad_maximum_fusion.6), channel_id=1, source_target_pairs={{0,1},{1,2},{2,3},{4,5},{5,6},{6,7},{8,9},{9,10},{10,11},{12,13},{... | collective-permute-start | bytes 1966088 | tf_op jit(solution)/shard_map/ppermute | solution.py:26
  109.2 7.1 %collective-permute-done.13 = bf16[4,80,1024]{2,1,0:T(8,128)(2,1)S(1)} collective-permute-done((bf16[4,80,1024]{2,1,0:T(8,128)(2,1)S(1)}, bf16[4,80,1024]{2,1,0:T(8,128)(2,1)S(1)}, u32[]{:S(2)}, u32[]{:S(2)}) %collective-permute-start.13) | collective-permute-done | bytes 655392 | tf_op jit(solution)/shard_map/ppermute | solution.py:26
  118.6 3.1 %fusion.4 = bf16[640,2048]{1,0:T(8,128)(2,1)S(1)} fusion(bf16[640,1024]{1,0:T(8,128)(2,1)S(1)} %bitcast.201, bf16[1,1,1024,2048]{3,2,1,0:T(8,128)(2,1)S(1)} %copy-done.17), kind=kOutput, calls=%fused_computation.4 | convolution fusion | flops 2685665280 | bytes 8126464 | tf_op jit(solution)/shard_map/dot_general | solution.py:245
  125.3 5.3 %collective-permute-start.19 = (bf16[2,80,2048]{2,1,0:T(8,128)(2,1)}, bf16[2,80,2048]{2,1,0:T(8,128)(2,1)}, u32[]{:S(2)}, u32[]{:S(2)}) collective-permute-start(bf16[2,80,2048]{2,1,0:T(8,128)(2,1)} %bitcast.46), channel_id=1, source_target_pairs={{0,1},{4,5},{8,9},{12,13},{16,17},{20,21},{24,25},{28,29}} | collective-permute-start | bytes 1966088 | tf_op jit(solution)/shard_map/ppermute | solution.py:26
  134.7 7.8 %collective-permute-done.19 = bf16[2,80,2048]{2,1,0:T(8,128)(2,1)} collective-permute-done((bf16[2,80,2048]{2,1,0:T(8,128)(2,1)}, bf16[2,80,2048]{2,1,0:T(8,128)(2,1)}, u32[]{:S(2)}, u32[]{:S(2)}) %collective-permute-start.19) | collective-permute-done | bytes 655392 | tf_op jit(solution)/shard_map/ppermute | solution.py:26
  142.5 3.0 %fusion.21 = (bf16[2,80,2048]{2,1,0:T(8,128)(2,1)}, bf16[2,80,2048]{2,1,0:T(8,128)(2,1)}) fusion(bf16[2,80,2048]{2,1,0:T(8,128)(2,1)} %bitcast.198, bf16[2,80,2048]{2,1,0:T(8,128)(2,1)} %collective-permute-done.20, bf16[2,80,2048]{2,1,0:T(8,128)(2,1)} %collective-permute-done.19), kind=kLoop, calls=%fused_computation.18 | loop fusion | flops 2293760 | bytes 3276800 | tf_op jit(solution)/shard_map/convert_element_type | solution.py:84
  147.0 5.0 %collective-permute-start.21 = (bf16[2,80,2048]{2,1,0:T(8,128)(2,1)}, bf16[2,80,2048]{2,1,0:T(8,128)(2,1)}, u32[]{:S(2)}, u32[]{:S(2)}) collective-permute-start(bf16[2,80,2048]{2,1,0:T(8,128)(2,1)} %get-tuple-element.115), channel_id=1, source_target_pairs={{0,1},{1,2},{4,5},{5,6},{8,9},{9,10},{12,13},{13,14},{16,17},{17,1... | collective-permute-start | bytes 1966088 | tf_op jit(solution)/shard_map/ppermute | solution.py:26
  157.1 6.0 %collective-permute-done.21 = bf16[2,80,2048]{2,1,0:T(8,128)(2,1)} collective-permute-done((bf16[2,80,2048]{2,1,0:T(8,128)(2,1)}, bf16[2,80,2048]{2,1,0:T(8,128)(2,1)}, u32[]{:S(2)}, u32[]{:S(2)}) %collective-permute-start.21) | collective-permute-done | bytes 655392 | tf_op jit(solution)/shard_map/ppermute | solution.py:26
  167.5 7.2 %collective-permute-start.23 = (bf16[2,80,2048]{2,1,0:T(8,128)(2,1)S(1)}, bf16[2,80,2048]{2,1,0:T(8,128)(2,1)S(1)}, u32[]{:S(2)}, u32[]{:S(2)}) collective-permute-start(bf16[2,80,2048]{2,1,0:T(8,128)(2,1)S(1)} %add_convert_fusion.1), channel_id=1, source_target_pairs={{0,1},{1,2},{2,3},{4,5},{5,6},{6,7},{8,9},{9,10},{10,11},{12,13},{... | collective-permute-start | bytes 1966088 | tf_op jit(solution)/shard_map/ppermute | solution.py:26
  178.0 2.9 %fusion.11 = bf16[640,1024]{1,0:T(8,128)(2,1)S(1)} fusion(bf16[640,2048]{1,0:T(8,128)(2,1)S(1)} %bitcast.196, bf16[1,1,1024,2048]{3,2,1,0:T(8,128)(2,1)S(1)} %copy-done.18), kind=kOutput, calls=%fused_computation.14 | convolution fusion | flops 2685009920 | bytes 8126464 | tf_op jit(solution)/shard_map/dot_general | solution.py:51
  181.6 4.9 %collective-permute-done.24 = bf16[2,80,2048]{2,1,0:T(8,128)(2,1)S(1)} collective-permute-done((bf16[2,80,2048]{2,1,0:T(8,128)(2,1)S(1)}, bf16[2,80,2048]{2,1,0:T(8,128)(2,1)S(1)}, u32[]{:S(2)}, u32[]{:S(2)}) %collective-permute-start.24) | collective-permute-done | bytes 655392 | tf_op jit(solution)/shard_map/ppermute | solution.py:26
  188.8 3.7 %collective-permute-start.26 = (bf16[2,80,1024]{2,1,0:T(8,128)(2,1)S(1)}, bf16[2,80,1024]{2,1,0:T(8,128)(2,1)S(1)}, u32[]{:S(2)}, u32[]{:S(2)}) collective-permute-start(bf16[2,80,1024]{2,1,0:T(8,128)(2,1)S(1)} %fusion.33), channel_id=1, source_target_pairs={{0,2},{1,3},{2,0},{3,1},{4,6},{5,7},{6,4},{7,5},{8,10},{9,11},{10,... | collective-permute-start | bytes 983048 | tf_op jit(solution)/shard_map/ppermute | solution.py:26
  194.7 2.4 collective-permute-done.31
  197.3 17.0 %collective-permute-done.26 = bf16[2,80,1024]{2,1,0:T(8,128)(2,1)S(1)} collective-permute-done((bf16[2,80,1024]{2,1,0:T(8,128)(2,1)S(1)}, bf16[2,80,1024]{2,1,0:T(8,128)(2,1)S(1)}, u32[]{:S(2)}, u32[]{:S(2)}) %collective-permute-start.26) | collective-permute-done | bytes 327712 | tf_op jit(solution)/shard_map/ppermute | solution.py:26
  220.1 3.9 %collective-permute-start.38 = (bf16[128,1024]{1,0:T(8,128)(2,1)S(1)}, bf16[128,1024]{1,0:T(8,128)(2,1)S(1)}, u32[]{:S(2)}, u32[]{:S(2)}) collective-permute-start(bf16[128,1024]{1,0:T(8,128)(2,1)S(1)} %get-tuple-element.110), channel_id=1, source_target_pairs={{0,25},{1,26},{2,27},{3,24},{4,29},{5,30},{6,31},{7,28},{8,1},{9,2... | collective-permute-start | bytes 786440 | tf_op jit(solution)/shard_map/ppermute | solution.py:26
  224.0 3.3 %collective-permute-start.37 = (bf16[128,1024]{1,0:T(8,128)(2,1)}, bf16[128,1024]{1,0:T(8,128)(2,1)}, u32[]{:S(2)}, u32[]{:S(2)}) collective-permute-start(bf16[128,1024]{1,0:T(8,128)(2,1)} %get-tuple-element.111), channel_id=1, source_target_pairs={{0,26},{1,27},{2,24},{3,25},{4,30},{5,31},{6,28},{7,29},{8,2},{9,3... | collective-permute-start | bytes 786440 | tf_op jit(solution)/shard_map/ppermute | solution.py:26
  227.3 3.2 %collective-permute-done.32 = bf16[4,80,1024]{2,1,0:T(8,128)(2,1)S(1)} collective-permute-done((bf16[4,80,1024]{2,1,0:T(8,128)(2,1)S(1)}, bf16[4,80,1024]{2,1,0:T(8,128)(2,1)S(1)}, u32[]{:S(2)}, u32[]{:S(2)}) %collective-permute-start.32) | collective-permute-done | bytes 655392 | tf_op jit(solution)/shard_map/ppermute | solution.py:26
  231.7 7.0 %collective-permute-start.33 = (bf16[128,1024]{1,0:T(8,128)(2,1)}, bf16[128,1024]{1,0:T(8,128)(2,1)}, u32[]{:S(2)}, u32[]{:S(2)}) collective-permute-start(bf16[128,1024]{1,0:T(8,128)(2,1)} %get-tuple-element.101), channel_id=1, source_target_pairs={{0,10},{1,11},{2,8},{3,9},{4,14},{5,15},{6,12},{7,13},{8,18},{9,19... | collective-permute-start | bytes 786440 | tf_op jit(solution)/shard_map/ppermute | solution.py:26
  239.4 17.5 %collective-permute-start.34 = (bf16[128,1024]{1,0:T(8,128)(2,1)}, bf16[128,1024]{1,0:T(8,128)(2,1)}, u32[]{:S(2)}, u32[]{:S(2)}) collective-permute-start(bf16[128,1024]{1,0:T(8,128)(2,1)} %get-tuple-element.102), channel_id=1, source_target_pairs={{0,9},{1,10},{2,11},{3,8},{4,13},{5,14},{6,15},{7,12},{8,17},{9,18... | collective-permute-start | bytes 786440 | tf_op jit(solution)/shard_map/ppermute | solution.py:26
  262.9 3.4 %finish.3 = bf16[1,128,4096]{2,1,0:T(8,128)(2,1)} custom-call(s32[4]{0:T(128)S(1)} %pad_add_fusion.2.at_ref, bf16[128,4096]{1,0:T(8,128)(2,1)S(1)} %copy-done.2, f32[128,1]{1,0:T(8,128)S(1)} %broadcast_in_dim_broadcast_in_dim.3.weight_ref, bf16[128,128]{1,0:T(8,128)(2,1)S(1)} %fusion.57.pick_ref, bf16[128,1024]{1,0:T(8,128)(2,1)} %collective-permute-done.37.refs_0_, ...), custom_call_target="tpu_custom_call" | custom-call | tf_op jit(solution)/shard_map/finish/pallas_call | solution.py:155
  268.6 3.4 %finish.2 = bf16[1,128,4096]{2,1,0:T(8,128)(2,1)} custom-call(s32[4]{0:T(128)S(1)} %pad_add_fusion.2.at_ref, bf16[128,4096]{1,0:T(8,128)(2,1)S(1)} %collective-permute-done.18.residual_ref, f32[128,1]{1,0:T(8,128)S(1)} %copy.22.weight_ref, bf16[128,128]{1,0:T(8,128)(2,1)S(1)} %fusion.56.pick_ref, bf16[128,1024]{1,0:T(8,128)(2,1)} %collective-permute-done.33.refs_0_, ...), custom_call_target="tpu_custom_call" | custom-call | tf_op jit(solution)/shard_map/finish/pallas_call | solution.py:155
  (169 shorter events, 84.2 us)
Async XLA Ops:
  10.9 26.8 %collective-permute-start.3 = (bf16[96,2048]{1,0:T(8,128)(2,1)}, bf16[96,2048]{1,0:T(8,128)(2,1)}, u32[]{:S(2)}, u32[]{:S(2)}) collective-permute-start(bf16[96,2048]{1,0:T(8,128)(2,1)} %pad_maximum_fusion.7), channel_id=1, source_target_pairs={{0,4},{1,5},{2,6},{3,7},{4,0},{5,1},{6,2},{7,3},{8,12},{9,13},{10,... | collective-permute-start | bytes 1179656 | tf_op jit(solution)/shard_map/ppermute | solution.py:26
  16.3 21.5 %collective-permute-start = (bf16[128,1024]{1,0:T(8,128)(2,1)}, bf16[128,1024]{1,0:T(8,128)(2,1)}, u32[]{:S(2)}, u32[]{:S(2)}) collective-permute-start(bf16[128,1024]{1,0:T(8,128)(2,1)} %convolution_convert_fusion.8), channel_id=1, source_target_pairs={{0,2},{1,3},{2,0},{3,1},{4,6},{5,7},{6,4},{7,5},{8,10},{9,11},{10,... | collective-permute-start | bytes 786440 | tf_op jit(solution)/shard_map/ppermute | solution.py:26
  19.8 17.9 %collective-permute-start.1 = (bf16[128,1024]{1,0:T(8,128)(2,1)}, bf16[128,1024]{1,0:T(8,128)(2,1)}, u32[]{:S(2)}, u32[]{:S(2)}) collective-permute-start(bf16[128,1024]{1,0:T(8,128)(2,1)} %convolution_convert_fusion.7), channel_id=1, source_target_pairs={{0,3},{1,0},{2,1},{3,2},{4,7},{5,4},{6,5},{7,6},{8,11},{9,8},{10,9... | collective-permute-start | bytes 786440 | tf_op jit(solution)/shard_map/ppermute | solution.py:26
  41.1 24.2 %collective-permute-start.8 = (bf16[128,1024]{1,0:T(8,128)(2,1)}, bf16[128,1024]{1,0:T(8,128)(2,1)S(1)}, u32[]{:S(2)}, u32[]{:S(2)}) collective-permute-start(bf16[128,1024]{1,0:T(8,128)(2,1)} %convolution_convert_fusion.3), channel_id=1, source_target_pairs={{0,2},{1,3},{2,0},{3,1},{4,6},{5,7},{6,4},{7,5},{8,10},{9,11},{10,... | collective-permute-start | bytes 786440 | tf_op jit(solution)/shard_map/ppermute | solution.py:26
  48.1 22.5 %collective-permute-start.9 = (bf16[128,1024]{1,0:T(8,128)(2,1)}, bf16[128,1024]{1,0:T(8,128)(2,1)S(1)}, u32[]{:S(2)}, u32[]{:S(2)}) collective-permute-start(bf16[128,1024]{1,0:T(8,128)(2,1)} %convolution_convert_fusion.4), channel_id=1, source_target_pairs={{0,3},{1,0},{2,1},{3,2},{4,7},{5,4},{6,5},{7,6},{8,11},{9,8},{10,9... | collective-permute-start | bytes 786440 | tf_op jit(solution)/shard_map/ppermute | solution.py:26
  48.6 22.0 %collective-permute-start.10 = (bf16[128,1024]{1,0:T(8,128)(2,1)}, bf16[128,1024]{1,0:T(8,128)(2,1)S(1)}, u32[]{:S(2)}, u32[]{:S(2)}) collective-permute-start(bf16[128,1024]{1,0:T(8,128)(2,1)} %convolution_convert_fusion.2), channel_id=1, source_target_pairs={{0,1},{1,2},{2,3},{3,0},{4,5},{5,6},{6,7},{7,4},{8,9},{9,10},{10,1... | collective-permute-start | bytes 786440 | tf_op jit(solution)/shard_map/ppermute | solution.py:26
  58.5 16.0 %collective-permute-start.7 = (bf16[2,80,1024]{2,1,0:T(8,128)(2,1)S(1)}, bf16[2,80,1024]{2,1,0:T(8,128)(2,1)S(1)}, u32[]{:S(2)}, u32[]{:S(2)}) collective-permute-start(bf16[2,80,1024]{2,1,0:T(8,128)(2,1)S(1)} %bitcast.211), channel_id=1, source_target_pairs={{0,3},{1,0},{2,1},{3,2},{4,7},{5,4},{6,5},{7,6},{8,11},{9,8},{10,9... | collective-permute-start | bytes 983048 | tf_op jit(solution)/shard_map/ppermute | solution.py:26
  62.8 21.4 %collective-permute-start.6 = (bf16[2,80,1024]{2,1,0:T(8,128)(2,1)S(1)}, bf16[2,80,1024]{2,1,0:T(8,128)(2,1)S(1)}, u32[]{:S(2)}, u32[]{:S(2)}) collective-permute-start(bf16[2,80,1024]{2,1,0:T(8,128)(2,1)S(1)} %bitcast.210), channel_id=1, source_target_pairs={{0,1},{1,2},{2,3},{3,0},{4,5},{5,6},{6,7},{7,4},{8,9},{9,10},{10,1... | collective-permute-start | bytes 983048 | tf_op jit(solution)/shard_map/ppermute | solution.py:26
  65.2 34.3 %collective-permute-start.5 = (bf16[2,80,1024]{2,1,0:T(8,128)(2,1)S(1)}, bf16[2,80,1024]{2,1,0:T(8,128)(2,1)S(1)}, u32[]{:S(2)}, u32[]{:S(2)}) collective-permute-start(bf16[2,80,1024]{2,1,0:T(8,128)(2,1)S(1)} %bitcast.209), channel_id=1, source_target_pairs={{0,2},{1,3},{2,0},{3,1},{4,6},{5,7},{6,4},{7,5},{8,10},{9,11},{10,... | collective-permute-start | bytes 983048 | tf_op jit(solution)/shard_map/ppermute | solution.py:26
  99.7 16.6 %collective-permute-start.13 = (bf16[4,80,1024]{2,1,0:T(8,128)(2,1)S(1)}, bf16[4,80,1024]{2,1,0:T(8,128)(2,1)S(1)}, u32[]{:S(2)}, u32[]{:S(2)}) collective-permute-start(bf16[4,80,1024]{2,1,0:T(8,128)(2,1)S(1)} %broadcast_select_fusion), channel_id=1, source_target_pairs={{0,4},{1,5},{2,6},{3,7},{4,0},{5,1},{6,2},{7,3},{8,12},{9,13},{10,... | collective-permute-start | bytes 1966088 | tf_op jit(solution)/shard_map/ppermute | solution.py:26
  102.8 19.0 %collective-permute-start.12 = (bf16[2,80,2048]{2,1,0:T(8,128)(2,1)S(1)}, bf16[2,80,2048]{2,1,0:T(8,128)(2,1)S(1)}, u32[]{:S(2)}, u32[]{:S(2)}) collective-permute-start(bf16[2,80,2048]{2,1,0:T(8,128)(2,1)S(1)} %pad_maximum_fusion.6), channel_id=1, source_target_pairs={{1,0},{2,1},{3,2},{5,4},{6,5},{7,6},{9,8},{10,9},{11,10},{13,12},{... | collective-permute-start | bytes 1966088 | tf_op jit(solution)/shard_map/ppermute | solution.py:26
  104.1 18.0 %collective-permute-start.11 = (bf16[2,80,2048]{2,1,0:T(8,128)(2,1)S(1)}, bf16[2,80,2048]{2,1,0:T(8,128)(2,1)S(1)}, u32[]{:S(2)}, u32[]{:S(2)}) collective-permute-start(bf16[2,80,2048]{2,1,0:T(8,128)(2,1)S(1)} %pad_maximum_fusion.6), channel_id=1, source_target_pairs={{0,1},{1,2},{2,3},{4,5},{5,6},{6,7},{8,9},{9,10},{10,11},{12,13},{... | collective-permute-start | bytes 1966088 | tf_op jit(solution)/shard_map/ppermute | solution.py:26
  125.3 17.2 %collective-permute-start.19 = (bf16[2,80,2048]{2,1,0:T(8,128)(2,1)}, bf16[2,80,2048]{2,1,0:T(8,128)(2,1)}, u32[]{:S(2)}, u32[]{:S(2)}) collective-permute-start(bf16[2,80,2048]{2,1,0:T(8,128)(2,1)} %bitcast.46), channel_id=1, source_target_pairs={{0,1},{4,5},{8,9},{12,13},{16,17},{20,21},{24,25},{28,29}} | collective-permute-start | bytes 1966088 | tf_op jit(solution)/shard_map/ppermute | solution.py:26
  130.5 22.7 %collective-permute-start.18 = (bf16[128,4096]{1,0:T(8,128)(2,1)}, bf16[128,4096]{1,0:T(8,128)(2,1)S(1)}, u32[]{:S(2)}, u32[]{:S(2)}) collective-permute-start(bf16[128,4096]{1,0:T(8,128)(2,1)} %bitcast.45), channel_id=1, source_target_pairs={{0,8},{1,9},{2,10},{3,11},{4,12},{5,13},{6,14},{7,15},{8,16},{9,17... | collective-permute-start | bytes 3145736 | tf_op jit(solution)/shard_map/ppermute | solution.py:26
  131.9 21.3 %collective-permute-start.16 = (bf16[2,80,2048]{2,1,0:T(8,128)(2,1)}, bf16[2,80,2048]{2,1,0:T(8,128)(2,1)}, u32[]{:S(2)}, u32[]{:S(2)}) collective-permute-start(bf16[2,80,2048]{2,1,0:T(8,128)(2,1)} %copy-done.13), channel_id=1, source_target_pairs={{1,2},{2,3},{5,6},{6,7},{9,10},{10,11},{13,14},{14,15},{17,18},{18... | collective-permute-start | bytes 1966088 | tf_op jit(solution)/shard_map/ppermute | solution.py:26
  133.4 19.8 %collective-permute-start.17 = (bf16[2,80,2048]{2,1,0:T(8,128)(2,1)}, bf16[2,80,2048]{2,1,0:T(8,128)(2,1)}, u32[]{:S(2)}, u32[]{:S(2)}) collective-permute-start(bf16[2,80,2048]{2,1,0:T(8,128)(2,1)} %copy-done.11), channel_id=1, source_target_pairs={{1,0},{2,1},{5,4},{6,5},{9,8},{10,9},{13,12},{14,13},{17,16},{18,1... | collective-permute-start | bytes 1966088 | tf_op jit(solution)/shard_map/ppermute | solution.py:26
  147.0 16.0 %collective-permute-start.21 = (bf16[2,80,2048]{2,1,0:T(8,128)(2,1)}, bf16[2,80,2048]{2,1,0:T(8,128)(2,1)}, u32[]{:S(2)}, u32[]{:S(2)}) collective-permute-start(bf16[2,80,2048]{2,1,0:T(8,128)(2,1)} %get-tuple-element.115), channel_id=1, source_target_pairs={{0,1},{1,2},{4,5},{5,6},{8,9},{9,10},{12,13},{13,14},{16,17},{17,1... | collective-permute-start | bytes 1966088 | tf_op jit(solution)/shard_map/ppermute | solution.py:26
  153.2 21.4 %collective-permute-start.28 = (bf16[2,80,2048]{2,1,0:T(8,128)(2,1)}, bf16[2,80,2048]{2,1,0:T(8,128)(2,1)S(1)}, u32[]{:S(2)}, u32[]{:S(2)}) collective-permute-start(bf16[2,80,2048]{2,1,0:T(8,128)(2,1)} %collective-permute-done.16), channel_id=1, source_target_pairs={{2,3},{6,7},{10,11},{14,15},{18,19},{22,23},{26,27},{30,31}} | collective-permute-start | bytes 1966088 | tf_op jit(solution)/shard_map/ppermute | solution.py:26
  153.9 20.7 %collective-permute-start.29 = (bf16[2,80,2048]{2,1,0:T(8,128)(2,1)}, bf16[2,80,2048]{2,1,0:T(8,128)(2,1)S(1)}, u32[]{:S(2)}, u32[]{:S(2)}) collective-permute-start(bf16[2,80,2048]{2,1,0:T(8,128)(2,1)} %collective-permute-done.17), channel_id=1, source_target_pairs={{1,0},{5,4},{9,8},{13,12},{17,16},{21,20},{25,24},{29,28}} | collective-permute-start | bytes 1966088 | tf_op jit(solution)/shard_map/ppermute | solution.py:26
  155.2 19.4 %collective-permute-start.30 = (bf16[128,4096]{1,0:T(8,128)(2,1)}, bf16[128,4096]{1,0:T(8,128)(2,1)S(1)}, u32[]{:S(2)}, u32[]{:S(2)}) collective-permute-start(bf16[128,4096]{1,0:T(8,128)(2,1)} %bitcast.207), channel_id=1, source_target_pairs={{0,24},{1,25},{2,26},{3,27},{4,28},{5,29},{6,30},{7,31},{8,0},{9,1... | collective-permute-start | bytes 3145736 | tf_op jit(solution)/shard_map/ppermute | solution.py:26
  164.5 22.0 %collective-permute-start.24 = (bf16[2,80,2048]{2,1,0:T(8,128)(2,1)S(1)}, bf16[2,80,2048]{2,1,0:T(8,128)(2,1)S(1)}, u32[]{:S(2)}, u32[]{:S(2)}) collective-permute-start(bf16[2,80,2048]{2,1,0:T(8,128)(2,1)S(1)} %add_convert_fusion), channel_id=1, source_target_pairs={{1,0},{2,1},{3,2},{5,4},{6,5},{7,6},{9,8},{10,9},{11,10},{13,12},{... | collective-permute-start | bytes 1966088 | tf_op jit(solution)/shard_map/ppermute | solution.py:26
  167.5 20.8 %collective-permute-start.23 = (bf16[2,80,2048]{2,1,0:T(8,128)(2,1)S(1)}, bf16[2,80,2048]{2,1,0:T(8,128)(2,1)S(1)}, u32[]{:S(2)}, u32[]{:S(2)}) collective-permute-start(bf16[2,80,2048]{2,1,0:T(8,128)(2,1)S(1)} %add_convert_fusion.1), channel_id=1, source_target_pairs={{0,1},{1,2},{2,3},{4,5},{5,6},{6,7},{8,9},{9,10},{10,11},{12,13},{... | collective-permute-start | bytes 1966088 | tf_op jit(solution)/shard_map/ppermute | solution.py:26
  181.0 16.1 %collective-permute-start.31 = (bf16[4,80,1024]{2,1,0:T(8,128)(2,1)S(1)}, bf16[4,80,1024]{2,1,0:T(8,128)(2,1)S(1)}, u32[]{:S(2)}, u32[]{:S(2)}) collective-permute-start(bf16[4,80,1024]{2,1,0:T(8,128)(2,1)S(1)} %dynamic-slice_bitcast_fusion.1), channel_id=1, source_target_pairs={{0,4},{1,5},{2,6},{3,7},{4,0},{5,1},{6,2},{7,3},{8,12},{9,13},{10,... | collective-permute-start | bytes 1966088 | tf_op jit(solution)/shard_map/ppermute | solution.py:26
  188.8 25.5 %collective-permute-start.26 = (bf16[2,80,1024]{2,1,0:T(8,128)(2,1)S(1)}, bf16[2,80,1024]{2,1,0:T(8,128)(2,1)S(1)}, u32[]{:S(2)}, u32[]{:S(2)}) collective-permute-start(bf16[2,80,1024]{2,1,0:T(8,128)(2,1)S(1)} %fusion.33), channel_id=1, source_target_pairs={{0,2},{1,3},{2,0},{3,1},{4,6},{5,7},{6,4},{7,5},{8,10},{9,11},{10,... | collective-permute-start | bytes 983048 | tf_op jit(solution)/shard_map/ppermute | solution.py:26
  192.5 21.8 %collective-permute-start.25 = (bf16[2,80,1024]{2,1,0:T(8,128)(2,1)S(1)}, bf16[2,80,1024]{2,1,0:T(8,128)(2,1)S(1)}, u32[]{:S(2)}, u32[]{:S(2)}) collective-permute-start(bf16[2,80,1024]{2,1,0:T(8,128)(2,1)S(1)} %fusion.33), channel_id=1, source_target_pairs={{0,3},{1,0},{2,1},{3,2},{4,7},{5,4},{6,5},{7,6},{8,11},{9,8},{10,9... | collective-permute-start | bytes 983048 | tf_op jit(solution)/shard_map/ppermute | solution.py:26
  193.7 20.6 %collective-permute-start.27 = (bf16[2,80,1024]{2,1,0:T(8,128)(2,1)S(1)}, bf16[2,80,1024]{2,1,0:T(8,128)(2,1)S(1)}, u32[]{:S(2)}, u32[]{:S(2)}) collective-permute-start(bf16[2,80,1024]{2,1,0:T(8,128)(2,1)S(1)} %fusion.33), channel_id=1, source_target_pairs={{0,1},{1,2},{2,3},{3,0},{4,5},{5,6},{6,7},{7,4},{8,9},{9,10},{10,1... | collective-permute-start | bytes 983048 | tf_op jit(solution)/shard_map/ppermute | solution.py:26
  217.8 20.9 %collective-permute-start.39 = (bf16[128,1024]{1,0:T(8,128)(2,1)S(1)}, bf16[128,1024]{1,0:T(8,128)(2,1)S(1)}, u32[]{:S(2)}, u32[]{:S(2)}) collective-permute-start(bf16[128,1024]{1,0:T(8,128)(2,1)S(1)} %get-tuple-element.109), channel_id=1, source_target_pairs={{0,27},{1,24},{2,25},{3,26},{4,31},{5,28},{6,29},{7,30},{8,3},{9,0... | collective-permute-start | bytes 786440 | tf_op jit(solution)/shard_map/ppermute | solution.py:26
  220.1 36.8 %collective-permute-start.38 = (bf16[128,1024]{1,0:T(8,128)(2,1)S(1)}, bf16[128,1024]{1,0:T(8,128)(2,1)S(1)}, u32[]{:S(2)}, u32[]{:S(2)}) collective-permute-start(bf16[128,1024]{1,0:T(8,128)(2,1)S(1)} %get-tuple-element.110), channel_id=1, source_target_pairs={{0,25},{1,26},{2,27},{3,24},{4,29},{5,30},{6,31},{7,28},{8,1},{9,2... | collective-permute-start | bytes 786440 | tf_op jit(solution)/shard_map/ppermute | solution.py:26
  224.0 35.8 %collective-permute-start.37 = (bf16[128,1024]{1,0:T(8,128)(2,1)}, bf16[128,1024]{1,0:T(8,128)(2,1)}, u32[]{:S(2)}, u32[]{:S(2)}) collective-permute-start(bf16[128,1024]{1,0:T(8,128)(2,1)} %get-tuple-element.111), channel_id=1, source_target_pairs={{0,26},{1,27},{2,24},{3,25},{4,30},{5,31},{6,28},{7,29},{8,2},{9,3... | collective-permute-start | bytes 786440 | tf_op jit(solution)/shard_map/ppermute | solution.py:26
  231.7 34.6 %collective-permute-start.36 = (bf16[128,1024]{1,0:T(8,128)(2,1)}, bf16[128,1024]{1,0:T(8,128)(2,1)}, u32[]{:S(2)}, u32[]{:S(2)}) collective-permute-start(bf16[128,1024]{1,0:T(8,128)(2,1)} %get-tuple-element.100), channel_id=1, source_target_pairs={{0,8},{1,9},{2,10},{3,11},{4,12},{5,13},{6,14},{7,15},{8,16},{9,17... | collective-permute-start | bytes 786440 | tf_op jit(solution)/shard_map/ppermute | solution.py:26
  231.7 34.6 %collective-permute-start.33 = (bf16[128,1024]{1,0:T(8,128)(2,1)}, bf16[128,1024]{1,0:T(8,128)(2,1)}, u32[]{:S(2)}, u32[]{:S(2)}) collective-permute-start(bf16[128,1024]{1,0:T(8,128)(2,1)} %get-tuple-element.101), channel_id=1, source_target_pairs={{0,10},{1,11},{2,8},{3,9},{4,14},{5,15},{6,12},{7,13},{8,18},{9,19... | collective-permute-start | bytes 786440 | tf_op jit(solution)/shard_map/ppermute | solution.py:26
  239.4 26.9 %collective-permute-start.34 = (bf16[128,1024]{1,0:T(8,128)(2,1)}, bf16[128,1024]{1,0:T(8,128)(2,1)}, u32[]{:S(2)}, u32[]{:S(2)}) collective-permute-start(bf16[128,1024]{1,0:T(8,128)(2,1)} %get-tuple-element.102), channel_id=1, source_target_pairs={{0,9},{1,10},{2,11},{3,8},{4,13},{5,14},{6,15},{7,12},{8,17},{9,18... | collective-permute-start | bytes 786440 | tf_op jit(solution)/shard_map/ppermute | solution.py:26
  (30 other events, 264.2 us)

commit v2 on v1

--- a/solution.py
+++ b/solution.py
@@ -10,15 +10,14 @@
 AXES = ("pp", "node", "local")
 
 
-def move(value, by_pp=0, by_node=0, by_local=0, wrap=True, first=0, last=None):
+def move(value, by_pp=0, by_node=0, by_local=0, wrap=True):
     pps, nodes, locs = (lax.axis_size(a) for a in AXES)
-    last = locs - 1 if last is None else last
     pairs = []
     for s in range(pps):
         for n in range(nodes):
             for l in range(locs):
                 to = l + by_local
-                if not wrap and not (first <= l <= last and 0 <= to < locs):
+                if not wrap and not 0 <= to < locs:
                     continue
                 source = (s * nodes + n) * locs + l
                 target = (((s + by_pp) % pps) * nodes + (n ^ by_node)) * locs + to % locs
@@ -65,54 +64,77 @@
     return lax.optimization_barrier(values)
 
 
-def after(values, *others):
-    return list(join(*values, *others)[: len(values)])
-
-
-def cut(tokens, placer, local):
-    column = tokens.shape[1] // 4
-    blocks = []
-    for m in range(4):
-        block = lax.dynamic_slice_in_dim(tokens, ((local - m) % 4) * column, column, axis=1)
-        blocks.append(jnp.dot(placer, block, preferred_element_type=F32).astype(BF16))
-    return blocks
-
-
-def sums(partial):
-    right, left = partial(3), partial(1)
-    for step in (1, 2, 3):
-        right, left = right.astype(BF16), left.astype(BF16)
-        got_r, got_l = yield (
-            (right, dict(by_local=1, wrap=False, last=step - 1)),
-            (left, dict(by_local=-1, wrap=False, first=4 - step)),
+def picker_of(route_ref):
+    tokens = route_ref.shape[1]
+    row = lax.broadcasted_iota(jnp.int32, (tokens, tokens), 0)
+    col = lax.broadcasted_iota(jnp.int32, (tokens, tokens), 1)
+    ones = route_ref[...].astype(F32)
+    before = jnp.dot(
+        jnp.broadcast_to(ones, (8, tokens)).astype(BF16),
+        (row < col).astype(BF16),
+        preferred_element_type=F32,
+    )[0:1]
+    zeros = tokens - jnp.sum(ones, axis=1, keepdims=True)
+    index = col[0:1].astype(F32)
+    place = jnp.where(ones == 0.0, index - before, zeros + before).astype(jnp.int32)
+    return (row == place).astype(BF16), zeros
+
+
+def cut_kernel(at_ref, route_ref, weight_ref, values_ref, *rest):
+    blocks = rest[-4:]
+    column = blocks[0].shape[1]
+    picker, zeros = picker_of(route_ref)
+    for i, block_ref in enumerate(blocks):
+        cols = pl.ds(pl.multiple_of(at_ref[i] * column, column), column)
+        block = (weight_ref[...] * values_ref[:, cols].astype(F32)).astype(BF16)
+        block_ref[...] = jnp.dot(picker, block, preferred_element_type=F32).astype(BF16)
+    if len(rest) > 4:
+        other_route_ref, saved_ref, own_ref, other_ref = rest[:4]
+        capacity, width = own_ref.shape
+        saved = jnp.dot(picker, saved_ref[...], preferred_element_type=F32)
+        low, high = saved[:capacity], saved[saved.shape[0] - capacity :]
+        first = at_ref[4] == 0
+        own_ref[...] = jnp.where(first, low, high).astype(BF16)
+        other_ref[:capacity] = jnp.where(first, high, low).astype(BF16)
+        zeros_other = other_route_ref.shape[1] - jnp.sum(
+            other_route_ref[...].astype(F32), axis=1, keepdims=True
         )
-        right = partial(3 - step).astype(F32) + got_r.astype(F32)
-        if step < 3:
-            left = partial(step + 1).astype(F32) + got_l.astype(F32)
-    yield right + got_l.astype(F32)
-
-
-def gathers(rows, local):
-    from_left, from_right = [rows], [rows]
-    for step in (1, 2, 3):
-        got_r, got_l = yield (
-            (from_left[-1], dict(by_local=1, wrap=False, first=step - 1)),
-            (from_right[-1], dict(by_local=-1, wrap=False, last=4 - step)),
-        )
-        from_left.append(got_r)
-        from_right.append(got_l)
-    slots = [rows]
-    for m in (1, 2, 3):
-        slots.append(jnp.where(local + m < 4, from_right[m], from_left[4 - m]))
-    yield jnp.stack(slots)
+        upper = lax.broadcasted_iota(jnp.int32, (16, width), 0) < 8
+        other_ref[capacity:] = jnp.where(upper, zeros_other, zeros).astype(BF16)
+
+
+def cut(tokens, weight, route, node, local, capacity, other_route=None, saved=None):
+    rows, features = tokens.shape
+    vmem = pl.BlockSpec(memory_space=pltpu.VMEM)
+    at = jnp.stack([(local - m) % 4 for m in range(4)] + [node]).astype(jnp.int32)
+    out_shape = [jax.ShapeDtypeStruct((rows, features // 4), BF16)] * 4
+    more = []
+    if saved is not None:
+        more = [other_route[None, :], saved]
+        width = saved.shape[1]
+        out_shape = [
+            jax.ShapeDtypeStruct((capacity, width), BF16),
+            jax.ShapeDtypeStruct((capacity + 16, width), BF16),
+        ] + out_shape
+    return list(
+        pl.pallas_call(
+            cut_kernel,
+            out_shape=out_shape,
+            in_specs=[pl.BlockSpec(memory_space=pltpu.SMEM)] + [vmem] * (3 + len(more)),
+            out_specs=[vmem] * len(out_shape),
+            compiler_params=pltpu.CompilerParams(vmem_limit_bytes=10 * 2**20),
+            name="cut",
+        )(at, route[None, :], weight[:, None], tokens, *more)
+    )
 
 
 def send(pieces):
     return [move(value, **how) for value, how in pieces]
 
 
-def operands(pieces):
-    return [value for value, _ in pieces]
+def both_ways(right, left):
+    right, left = right.astype(BF16), left.astype(BF16)
+    return move(right, by_local=1, wrap=False), move(left, by_local=-1, wrap=False)
 
 
 def valid(zeros, node, tokens, capacity):
@@ -180,7 +202,6 @@
 
     act, grad = act_fwd[0], grad_bwd[0]
     route_a, route_b = routes_fwd[0, :, 0], routes_bwd[0, :, 0]
-    sort_a = sorter(route_a)
     zeros = tokens_here - jnp.stack([jnp.sum(route_a), jnp.sum(route_b)]).astype(F32)
 
     def in_rows(cuts, got):
@@ -194,24 +215,14 @@
         other = lax.dynamic_index_in_dim(done, 1 - node, axis=1, keepdims=False)
         return own, other
 
-    def turn(chain, back, *others):
-        pieces = chain.send(after(back, *others))
-        return operands(pieces), send(pieces)
-
-    dy = (weight_bwd[0][:, None] * grad.astype(F32)).astype(BF16)
-    sort_b = sorter(route_b)
-    cut_b = cut(dy, sort_b, local)
+    saved_own, saved_other, *cut_b = cut(
+        grad, weight_bwd[0], route_b, node, local, capacity, route_a, saved_bwd[0]
+    )
     got_b = [move(cut_b[m], by_local=-m) for m in (2, 1, 3)]
-    saved = jnp.dot(sort_b, saved_bwd[0], preferred_element_type=F32).astype(BF16)
-    saved_own, saved_other = windows(saved, node, capacity)
-    extra = jnp.broadcast_to(jnp.repeat(zeros, 8)[:, None], (16, saved.shape[1])).astype(BF16)
-    saved_got = move(jnp.concatenate([saved_other, extra], axis=0), by_node=1)
-    cut_a = cut(act, sort_a, local)
+    saved_got = move(saved_other, by_node=1)
+    cut_a = cut(act, jnp.ones((tokens_here,), F32), route_a, node, local, capacity)
     *got_b, saved_got, a0, a1, a2, a3 = join(*got_b, saved_got, *cut_a)
     cut_a = [a0, a1, a2, a3]
-    zeros_got = saved_got[capacity::8, 0].astype(F32)
-    saved_got = saved_got[:capacity]
-    zeros = by_node(zeros, zeros_got, 0)
     got_a = [move(cut_a[m], by_local=-m) for m in (2, 1, 3)]
     own_b, other_b = in_rows(cut_b, got_b)
     column = own_b.shape[-1]
@@ -222,6 +233,9 @@
     back_b = [move(part_b[m], by_local=m) for m in (2, 1, 3)]
     both = join(*back_b, *got_a)
     back_b, got_a = both[:3], both[3:]
+    zeros_got = saved_got[capacity::8, 0].astype(F32)
+    saved_got = saved_got[:capacity]
+    zeros = by_node(zeros, zeros_got, 0)
     own_a, other_a = in_rows(cut_a, got_a)
     got_ax = move(other_a, by_node=1)
     dh = part_b[0].astype(F32) + sum(part.astype(F32) for part in back_b)
@@ -234,34 +248,52 @@
         BF16
     )
 
-    chain_b = gathers(grad_gu, local)
-    back_b = send(next(chain_b))
-    small_wait, route_wait = after(
-        [jnp.stack([route_a.astype(F32), weight_fwd[0]]), route_b], grad_gu
-    )
-    small_next = move(small_wait, by_pp=1)
-    route_b_next = move(route_wait, by_pp=-1)
+    small = jnp.stack([route_a.astype(F32), weight_fwd[0]])
+    grad_gu, small, route_next = join(grad_gu, small, route_b)
+    got_r, got_l = both_ways(grad_gu, grad_gu)
+    small_next = move(small, by_pp=1)
+    route_b_next = move(route_next, by_pp=-1)
     rows_a = by_node(own_a, got_ax, 1).reshape(-1, column)
     part_a = jnp.dot(rows_a, w_gu, preferred_element_type=F32).astype(BF16)
-    *back_b, part_a, small_next, route_b_next = join(*back_b, part_a, small_next, route_b_next)
+    got_r, got_l, part_a, small_next, route_b_next, act_in, grad_in = join(
+        got_r, got_l, part_a, small_next, route_b_next, act, grad
+    )
     part_a = part_a.reshape(shape + (2 * hidden_units,))
-    chain_a = sums(lambda slot: part_a[slot])
-    values_b, back_b = turn(chain_b, back_b)
-    pieces = next(chain_a)
-    back_a = send(pieces)
-    act_next = move(after([act], *operands(pieces))[0], by_pp=1)
-    *back_b, act_next = join(*back_b, act_next)
-    values_b, back_b = turn(chain_b, back_b)
-    grad_next = move(join(grad, *values_b)[0], by_pp=-1)
-    *back_b, grad_next = join(*back_b, grad_next)
-    values_a, back_a = turn(chain_a, back_a)
-    values_a, back_a = turn(chain_a, back_a)
-    all_gu = chain_b.send(back_b)
+    lefts, rights = [grad_gu, got_r], [grad_gu, got_l]
+
+    got_r, got_l = both_ways(
+        jnp.where(local == 0, part_a[3], got_r),
+        jnp.where(local == 3, part_a[1], got_l),
+    )
+    act_next = move(act_in, by_pp=1)
+    got_r, got_l, act_next, grad_in = join(got_r, got_l, act_next, grad_in)
+    lefts.append(got_r)
+    rights.append(got_l)
+
+    got_r, got_l = got_r.astype(F32), got_l.astype(F32)
+    got_r, got_l = both_ways(
+        jnp.where(local == 2, 0.0, part_a[2].astype(F32)) + jnp.where(local == 0, 0.0, got_r),
+        jnp.where(local == 1, 0.0, part_a[2].astype(F32)) + jnp.where(local == 3, 0.0, got_l),
+    )
+    grad_next = move(grad_in, by_pp=-1)
+    got_r, got_l, grad_next = join(got_r, got_l, grad_next)
+    lefts.append(got_r)
+    rights.append(got_l)
+
+    middle = (local == 1) | (local == 2)
+    got_r, got_l = both_ways(
+        part_a[1].astype(F32) + jnp.where(middle, got_r.astype(F32), 0.0),
+        part_a[3].astype(F32) + jnp.where(middle, got_l.astype(F32), 0.0),
+    )
+    preact = part_a[0].astype(F32) + got_r.astype(F32) + got_l.astype(F32)
+
+    all_gu = jnp.stack(
+        [grad_gu] + [jnp.where(local + m < 4, rights[m], lefts[4 - m]) for m in (1, 2, 3)]
+    )
     done_b = dot_t(all_gu.reshape(-1, 2 * hidden_units), w_gu).astype(BF16)
     own_b, other_b = split(done_b.reshape(shape + (column,)))
     got_b = move(other_b, by_node=1)
 
-    preact = chain_a.send(back_a)
     preact = jnp.where(valid(zeros[:, 0], node, tokens_here, capacity)[..., None], preact, 0.0)
     hidden = (jax.nn.silu(preact[..., :hidden_units]) * preact[..., hidden_units:]).astype(BF16)
     all_hidden = [move(hidden, by_local=-m) for m in (1, 2, 3)]

time: 274 us -> 278 us (1.015)
  waiting for transfers between devices: 93.7 us -> 121 us
  starting transfers between devices: 104 us -> 90.1 us
  matrix products: 21.6 us -> 9.39 us
  Pallas kernels: 6.74 us -> 10.3 us
    ppermute x41 -> x37, waiting for transfers between devices: 93.7 us -> 121 us  [move(): return lax.ppermute(value, AXES, pairs)]
    ppermute x41 -> x37, starting transfers between devices: 104 us -> 90.1 us  [move(): return lax.ppermute(value, AXES, pairs)]
    dot_general x9 -> x0, matrix products: 11.2 us -> none  [the longest x8 9.83 us: cut(): jnp.dot(placer, block, preferred_element_type=F32).astype(BF16)]
    select_n x0 -> x3, other arithmetic: none -> 3.34 us  [the longest x1 1.39 us: body_pair(): jnp.where(local == 1, 0.0, part_a[2].astype(F32))]
    pallas_call x0 -> x2, Pallas kernels: none -> 3.08 us  [cut(): pl.pallas_call(cut_kernel, out_shape=out_shape, in_specs=[pl.BlockSpec(me...]
    convert_element_type x6 -> x5, other arithmetic: 10.2 us -> 7.7 us  [the longest x4 7.04 us: both_ways(): right, left = (right.astype(BF16), left.astype(BF16))]
    unnamed x42 -> x66, local copies, waits for them, and re-layouts: 10.9 us -> 12.5 us
  transfers between devices with their start and end apart: 41 -> 37, of which waited for: 16 -> 17; matrix products, arithmetic and copies ran while one was open for 14% -> 11% of each run, Pallas kernels for 1% -> 2%
where the time goes in v2:
time: 278 us; the launch traced here: 276 us
  waiting for transfers between devices  121 us (44%)
  starting transfers between devices  90.1 us (32%)
  other arithmetic  25.6 us (9%)
  local copies, waits for them, and re-layouts  17 us (6%)
  Pallas kernels  10.3 us (4%)
  matrix products  9.39 us (3%)
  between operations  2.84 us (1%)
    ppermute x37, waiting for transfers between devices, move(): return lax.ppermute(value, AXES, pairs)  121 us
    ppermute x37, starting transfers between devices, move(): return lax.ppermute(value, AXES, pairs)  90.1 us
    unnamed x66, local copies, waits for them, and re-layouts  12.5 us
    pallas_call x2, Pallas kernels, finish(): pl.pallas_call(finish_kernel, out_shape=jax.ShapeDtypeStruct((1, tokens,...  7.25 us
    convert_element_type x4, other arithmetic, both_ways(): right, left = (right.astype(BF16), left.astype(BF16))  7.04 us
  transfers between devices with their start and end apart: 37, of which 17 were waited for; matrix products, arithmetic and copies ran while one was open for 11% of the time, Pallas kernels for 2%

profile of v2, /device:TPU:0, one launch (start us, length us, event | category | flops | bytes accessed | tf_op | source)
XLA Modules:
  0.0 276.0 jit_solution(8278697475773005219)
XLA Ops:
  8.1 2.9 %collective-permute-start.3 = (bf16[96,2048]{1,0:T(8,128)(2,1)}, bf16[96,2048]{1,0:T(8,128)(2,1)}, u32[]{:S(2)}, u32[]{:S(2)}) collective-permute-start(bf16[96,2048]{1,0:T(8,128)(2,1)} %get-tuple-element.50), channel_id=1, source_target_pairs={{0,4},{1,5},{2,6},{3,7},{4,0},{5,1},{6,2},{7,3},{8,12},{9,13},{10,... | collective-permute-start | bytes 1179656 | tf_op jit(solution)/shard_map/ppermute | solution.py:25
  20.9 11.5 %collective-permute-done = bf16[128,1024]{1,0:T(8,128)(2,1)} collective-permute-done((bf16[128,1024]{1,0:T(8,128)(2,1)}, bf16[128,1024]{1,0:T(8,128)(2,1)}, u32[]{:S(2)}, u32[]{:S(2)}) %collective-permute-start) | collective-permute-done | bytes 262176 | tf_op jit(solution)/shard_map/ppermute | solution.py:25
  36.8 7.1 %collective-permute-start.8 = (bf16[128,1024]{1,0:T(8,128)(2,1)}, bf16[128,1024]{1,0:T(8,128)(2,1)S(1)}, u32[]{:S(2)}, u32[]{:S(2)}) collective-permute-start(bf16[128,1024]{1,0:T(8,128)(2,1)} %copy-done.15), channel_id=1, source_target_pairs={{0,2},{1,3},{2,0},{3,1},{4,6},{5,7},{6,4},{7,5},{8,10},{9,11},{10,... | collective-permute-start | bytes 786440 | tf_op jit(solution)/shard_map/ppermute | solution.py:25
  47.1 4.0 %collective-permute-done.4 = bf16[4,80,1024]{2,1,0:T(8,128)(2,1)} collective-permute-done((bf16[4,80,1024]{2,1,0:T(8,128)(2,1)}, bf16[4,80,1024]{2,1,0:T(8,128)(2,1)}, u32[]{:S(2)}, u32[]{:S(2)}) %collective-permute-start.4) | collective-permute-done | bytes 655392 | tf_op jit(solution)/shard_map/ppermute | solution.py:25
  54.3 3.8 %collective-permute-start.7 = (bf16[2,80,1024]{2,1,0:T(8,128)(2,1)S(1)}, bf16[2,80,1024]{2,1,0:T(8,128)(2,1)S(1)}, u32[]{:S(2)}, u32[]{:S(2)}) collective-permute-start(bf16[2,80,1024]{2,1,0:T(8,128)(2,1)S(1)} %bitcast.178), channel_id=1, source_target_pairs={{0,3},{1,0},{2,1},{3,2},{4,7},{5,4},{6,5},{7,6},{8,11},{9,8},{10,9... | collective-permute-start | bytes 983048 | tf_op jit(solution)/shard_map/ppermute | solution.py:25
  58.1 2.8 %collective-permute-start.6 = (bf16[2,80,1024]{2,1,0:T(8,128)(2,1)S(1)}, bf16[2,80,1024]{2,1,0:T(8,128)(2,1)S(1)}, u32[]{:S(2)}, u32[]{:S(2)}) collective-permute-start(bf16[2,80,1024]{2,1,0:T(8,128)(2,1)S(1)} %bitcast.177), channel_id=1, source_target_pairs={{0,1},{1,2},{2,3},{3,0},{4,5},{5,6},{6,7},{7,4},{8,9},{9,10},{10,1... | collective-permute-start | bytes 983048 | tf_op jit(solution)/shard_map/ppermute | solution.py:25
  61.0 3.9 %collective-permute-start.5 = (bf16[2,80,1024]{2,1,0:T(8,128)(2,1)S(1)}, bf16[2,80,1024]{2,1,0:T(8,128)(2,1)S(1)}, u32[]{:S(2)}, u32[]{:S(2)}) collective-permute-start(bf16[2,80,1024]{2,1,0:T(8,128)(2,1)S(1)} %bitcast.176), channel_id=1, source_target_pairs={{0,2},{1,3},{2,0},{3,1},{4,6},{5,7},{6,4},{7,5},{8,10},{9,11},{10,... | collective-permute-start | bytes 983048 | tf_op jit(solution)/shard_map/ppermute | solution.py:25
  66.4 3.9 %collective-permute-done.7 = bf16[2,80,1024]{2,1,0:T(8,128)(2,1)S(1)} collective-permute-done((bf16[2,80,1024]{2,1,0:T(8,128)(2,1)S(1)}, bf16[2,80,1024]{2,1,0:T(8,128)(2,1)S(1)}, u32[]{:S(2)}, u32[]{:S(2)}) %collective-permute-start.7) | collective-permute-done | bytes 327712 | tf_op jit(solution)/shard_map/ppermute | solution.py:25
  70.3 9.7 %collective-permute-done.6 = bf16[2,80,1024]{2,1,0:T(8,128)(2,1)S(1)} collective-permute-done((bf16[2,80,1024]{2,1,0:T(8,128)(2,1)S(1)}, bf16[2,80,1024]{2,1,0:T(8,128)(2,1)S(1)}, u32[]{:S(2)}, u32[]{:S(2)}) %collective-permute-start.6) | collective-permute-done | bytes 327712 | tf_op jit(solution)/shard_map/ppermute | solution.py:25
  80.0 15.3 %collective-permute-done.5 = bf16[2,80,1024]{2,1,0:T(8,128)(2,1)S(1)} collective-permute-done((bf16[2,80,1024]{2,1,0:T(8,128)(2,1)S(1)}, bf16[2,80,1024]{2,1,0:T(8,128)(2,1)S(1)}, u32[]{:S(2)}, u32[]{:S(2)}) %collective-permute-start.5) | collective-permute-done | bytes 327712 | tf_op jit(solution)/shard_map/ppermute | solution.py:25
  99.1 4.6 %collective-permute-start.11 = (bf16[2,80,2048]{2,1,0:T(8,128)(2,1)S(1)}, bf16[2,80,2048]{2,1,0:T(8,128)(2,1)S(1)}, u32[]{:S(2)}, u32[]{:S(2)}) collective-permute-start(bf16[2,80,2048]{2,1,0:T(8,128)(2,1)S(1)} %pad_maximum_fusion.6), channel_id=1, source_target_pairs={{0,1},{1,2},{2,3},{4,5},{5,6},{6,7},{8,9},{9,10},{10,11},{12,13},{... | collective-permute-start | bytes 1966088 | tf_op jit(solution)/shard_map/ppermute | solution.py:25
  104.2 7.8 %collective-permute-done.13 = bf16[4,80,1024]{2,1,0:T(8,128)(2,1)S(1)} collective-permute-done((bf16[4,80,1024]{2,1,0:T(8,128)(2,1)S(1)}, bf16[4,80,1024]{2,1,0:T(8,128)(2,1)S(1)}, u32[]{:S(2)}, u32[]{:S(2)}) %collective-permute-start.13) | collective-permute-done | bytes 655392 | tf_op jit(solution)/shard_map/ppermute | solution.py:25
  114.4 3.1 %fusion.4 = bf16[640,2048]{1,0:T(8,128)(2,1)S(1)} fusion(bf16[640,1024]{1,0:T(8,128)(2,1)S(1)} %bitcast.170, bf16[1,1,1024,2048]{3,2,1,0:T(8,128)(2,1)S(1)} %copy-done.31), kind=kOutput, calls=%fused_computation.4 | convolution fusion | flops 2685665280 | bytes 8126464 | tf_op jit(solution)/shard_map/dot_general | solution.py:257
  120.4 4.0 %collective-permute-start.16 = (bf16[2,80,2048]{2,1,0:T(8,128)(2,1)}, bf16[2,80,2048]{2,1,0:T(8,128)(2,1)}, u32[]{:S(2)}, u32[]{:S(2)}) collective-permute-start(bf16[2,80,2048]{2,1,0:T(8,128)(2,1)} %broadcast_select_fusion.5), channel_id=1, source_target_pairs={{0,1},{1,2},{2,3},{4,5},{5,6},{6,7},{8,9},{9,10},{10,11},{12,13},{... | collective-permute-start | bytes 1966088 | tf_op jit(solution)/shard_map/ppermute | solution.py:25
  129.5 8.9 %collective-permute-done.16 = bf16[2,80,2048]{2,1,0:T(8,128)(2,1)} collective-permute-done((bf16[2,80,2048]{2,1,0:T(8,128)(2,1)}, bf16[2,80,2048]{2,1,0:T(8,128)(2,1)}, u32[]{:S(2)}, u32[]{:S(2)}) %collective-permute-start.16) | collective-permute-done | bytes 655392 | tf_op jit(solution)/shard_map/ppermute | solution.py:25
  138.4 6.5 %collective-permute-done.17 = bf16[2,80,2048]{2,1,0:T(8,128)(2,1)} collective-permute-done((bf16[2,80,2048]{2,1,0:T(8,128)(2,1)}, bf16[2,80,2048]{2,1,0:T(8,128)(2,1)}, u32[]{:S(2)}, u32[]{:S(2)}) %collective-permute-start.17) | collective-permute-done | bytes 655392 | tf_op jit(solution)/shard_map/ppermute | solution.py:25
  155.5 7.9 %collective-permute-done.19 = bf16[2,80,2048]{2,1,0:T(8,128)(2,1)} collective-permute-done((bf16[2,80,2048]{2,1,0:T(8,128)(2,1)}, bf16[2,80,2048]{2,1,0:T(8,128)(2,1)}, u32[]{:S(2)}, u32[]{:S(2)}) %collective-permute-start.19) | collective-permute-done | bytes 655392 | tf_op jit(solution)/shard_map/ppermute | solution.py:25
  163.4 7.4 %collective-permute-done.20 = bf16[2,80,2048]{2,1,0:T(8,128)(2,1)} collective-permute-done((bf16[2,80,2048]{2,1,0:T(8,128)(2,1)}, bf16[2,80,2048]{2,1,0:T(8,128)(2,1)}, u32[]{:S(2)}, u32[]{:S(2)}) %collective-permute-start.20) | collective-permute-done | bytes 655392 | tf_op jit(solution)/shard_map/ppermute | solution.py:25
  175.1 4.8 %collective-permute-start.22 = (bf16[2,80,2048]{2,1,0:T(8,128)(2,1)S(1)}, bf16[2,80,2048]{2,1,0:T(8,128)(2,1)S(1)}, u32[]{:S(2)}, u32[]{:S(2)}) collective-permute-start(bf16[2,80,2048]{2,1,0:T(8,128)(2,1)S(1)} %add_convert_fusion.1), channel_id=1, source_target_pairs={{0,1},{1,2},{2,3},{4,5},{5,6},{6,7},{8,9},{9,10},{10,11},{12,13},{... | collective-permute-start | bytes 1966088 | tf_op jit(solution)/shard_map/ppermute | solution.py:25
  183.4 2.9 %fusion.11 = bf16[640,1024]{1,0:T(8,128)(2,1)S(1)} fusion(bf16[640,2048]{1,0:T(8,128)(2,1)S(1)} %bitcast.166, bf16[1,1,1024,2048]{3,2,1,0:T(8,128)(2,1)S(1)} %copy-done.32), kind=kOutput, calls=%fused_computation.12 | convolution fusion | flops 2685009920 | bytes 8126464 | tf_op jit(solution)/shard_map/dot_general | solution.py:50
  187.0 5.0 %collective-permute-done.23 = bf16[2,80,2048]{2,1,0:T(8,128)(2,1)S(1)} collective-permute-done((bf16[2,80,2048]{2,1,0:T(8,128)(2,1)S(1)}, bf16[2,80,2048]{2,1,0:T(8,128)(2,1)S(1)}, u32[]{:S(2)}, u32[]{:S(2)}) %collective-permute-start.23) | collective-permute-done | bytes 655392 | tf_op jit(solution)/shard_map/ppermute | solution.py:25
  198.6 3.6 %collective-permute-done.27 = bf16[4,80,1024]{2,1,0:T(8,128)(2,1)S(1)} collective-permute-done((bf16[4,80,1024]{2,1,0:T(8,128)(2,1)S(1)}, bf16[4,80,1024]{2,1,0:T(8,128)(2,1)S(1)}, u32[]{:S(2)}, u32[]{:S(2)}) %collective-permute-start.27) | collective-permute-done | bytes 655392 | tf_op jit(solution)/shard_map/ppermute | solution.py:25
  202.6 16.2 %collective-permute-done.25 = bf16[2,80,1024]{2,1,0:T(8,128)(2,1)S(1)} collective-permute-done((bf16[2,80,1024]{2,1,0:T(8,128)(2,1)S(1)}, bf16[2,80,1024]{2,1,0:T(8,128)(2,1)S(1)}, u32[]{:S(2)}, u32[]{:S(2)}) %collective-permute-start.25) | collective-permute-done | bytes 327712 | tf_op jit(solution)/shard_map/ppermute | solution.py:25
  223.2 4.0 %collective-permute-start.34 = (bf16[128,1024]{1,0:T(8,128)(2,1)S(1)}, bf16[128,1024]{1,0:T(8,128)(2,1)S(1)}, u32[]{:S(2)}, u32[]{:S(2)}) collective-permute-start(bf16[128,1024]{1,0:T(8,128)(2,1)S(1)} %get-tuple-element.119), channel_id=1, source_target_pairs={{0,25},{1,26},{2,27},{3,24},{4,29},{5,30},{6,31},{7,28},{8,1},{9,2... | collective-permute-start | bytes 786440 | tf_op jit(solution)/shard_map/ppermute | solution.py:25
  227.2 4.1 %collective-permute-start.33 = (bf16[128,1024]{1,0:T(8,128)(2,1)}, bf16[128,1024]{1,0:T(8,128)(2,1)S(1)}, u32[]{:S(2)}, u32[]{:S(2)}) collective-permute-start(bf16[128,1024]{1,0:T(8,128)(2,1)} %get-tuple-element.120), channel_id=1, source_target_pairs={{0,26},{1,27},{2,24},{3,25},{4,30},{5,31},{6,28},{7,29},{8,2},{9,3... | collective-permute-start | bytes 786440 | tf_op jit(solution)/shard_map/ppermute | solution.py:25
  231.3 3.5 %collective-permute-done.28 = bf16[4,80,1024]{2,1,0:T(8,128)(2,1)S(1)} collective-permute-done((bf16[4,80,1024]{2,1,0:T(8,128)(2,1)S(1)}, bf16[4,80,1024]{2,1,0:T(8,128)(2,1)S(1)}, u32[]{:S(2)}, u32[]{:S(2)}) %collective-permute-start.28) | collective-permute-done | bytes 655392 | tf_op jit(solution)/shard_map/ppermute | solution.py:25
  235.9 7.2 %collective-permute-start.29 = (bf16[128,1024]{1,0:T(8,128)(2,1)}, bf16[128,1024]{1,0:T(8,128)(2,1)}, u32[]{:S(2)}, u32[]{:S(2)}) collective-permute-start(bf16[128,1024]{1,0:T(8,128)(2,1)} %get-tuple-element.110), channel_id=1, source_target_pairs={{0,10},{1,11},{2,8},{3,9},{4,14},{5,15},{6,12},{7,13},{8,18},{9,19... | collective-permute-start | bytes 786440 | tf_op jit(solution)/shard_map/ppermute | solution.py:25
  243.1 16.8 %collective-permute-start.30 = (bf16[128,1024]{1,0:T(8,128)(2,1)}, bf16[128,1024]{1,0:T(8,128)(2,1)}, u32[]{:S(2)}, u32[]{:S(2)}) collective-permute-start(bf16[128,1024]{1,0:T(8,128)(2,1)} %get-tuple-element.111), channel_id=1, source_target_pairs={{0,9},{1,10},{2,11},{3,8},{4,13},{5,14},{6,15},{7,12},{8,17},{9,18... | collective-permute-start | bytes 786440 | tf_op jit(solution)/shard_map/ppermute | solution.py:25
  260.2 3.7 %collective-permute-done.33.refs_0_ = bf16[128,1024]{1,0:T(8,128)(2,1)S(1)} collective-permute-done((bf16[128,1024]{1,0:T(8,128)(2,1)}, bf16[128,1024]{1,0:T(8,128)(2,1)S(1)}, u32[]{:S(2)}, u32[]{:S(2)}) %collective-permute-start.33) | collective-permute-done | bytes 262176 | tf_op jit(solution)/shard_map/ppermute | solution.py:25
  264.0 3.2 %finish.3 = bf16[1,128,4096]{2,1,0:T(8,128)(2,1)} custom-call(s32[4]{0:T(128)S(1)} %pad_add_fusion.2.at_ref, bf16[128,4096]{1,0:T(8,128)(2,1)} %collective-permute-done.21.residual_ref, f32[128,1]{1,0:T(8,128)S(1)} %broadcast_12_weight_ref.2.weight_ref, bf16[128,128]{1,0:T(8,128)(2,1)S(1)} %fusion.41.pick_ref, ...), custom_call_target="tpu_custom_call" | custom-call | tf_op jit(solution)/shard_map/finish/pallas_call | solution.py:177
  267.2 4.6 %collective-permute-done.31.refs_2_ = bf16[128,1024]{1,0:T(8,128)(2,1)} collective-permute-done((bf16[128,1024]{1,0:T(8,128)(2,1)}, bf16[128,1024]{1,0:T(8,128)(2,1)}, u32[]{:S(2)}, u32[]{:S(2)}) %collective-permute-start.31) | collective-permute-done | bytes 262176 | tf_op jit(solution)/shard_map/ppermute | solution.py:25
  271.8 4.1 %finish.2 = bf16[1,128,4096]{2,1,0:T(8,128)(2,1)} custom-call(s32[4]{0:T(128)S(1)} %pad_add_fusion.2.at_ref, bf16[128,4096]{1,0:T(8,128)(2,1)} %collective-permute-done.18.residual_ref, f32[128,1]{1,0:T(8,128)S(1)} %copy.24.weight_ref, bf16[128,128]{1,0:T(8,128)(2,1)S(1)} %fusion.40.pick_ref, bf16[128,1024]{1,0:T(8,128)(2,1)} %collective-permute-done.29.refs_0_, ...), custom_call_target="tpu_custom_call" | custom-call | tf_op jit(solution)/shard_map/finish/pallas_call | solution.py:177
  (173 shorter events, 74.3 us)
Async XLA Ops:
  8.1 24.4 %collective-permute-start.3 = (bf16[96,2048]{1,0:T(8,128)(2,1)}, bf16[96,2048]{1,0:T(8,128)(2,1)}, u32[]{:S(2)}, u32[]{:S(2)}) collective-permute-start(bf16[96,2048]{1,0:T(8,128)(2,1)} %get-tuple-element.50), channel_id=1, source_target_pairs={{0,4},{1,5},{2,6},{3,7},{4,0},{5,1},{6,2},{7,3},{8,12},{9,13},{10,... | collective-permute-start | bytes 1179656 | tf_op jit(solution)/shard_map/ppermute | solution.py:25
  11.0 21.4 %collective-permute-start = (bf16[128,1024]{1,0:T(8,128)(2,1)}, bf16[128,1024]{1,0:T(8,128)(2,1)}, u32[]{:S(2)}, u32[]{:S(2)}) collective-permute-start(bf16[128,1024]{1,0:T(8,128)(2,1)} %get-tuple-element.47), channel_id=1, source_target_pairs={{0,2},{1,3},{2,0},{3,1},{4,6},{5,7},{6,4},{7,5},{8,10},{9,11},{10,... | collective-permute-start | bytes 786440 | tf_op jit(solution)/shard_map/ppermute | solution.py:25
  13.6 18.8 %collective-permute-start.1 = (bf16[128,1024]{1,0:T(8,128)(2,1)}, bf16[128,1024]{1,0:T(8,128)(2,1)}, u32[]{:S(2)}, u32[]{:S(2)}) collective-permute-start(bf16[128,1024]{1,0:T(8,128)(2,1)} %get-tuple-element.48), channel_id=1, source_target_pairs={{0,3},{1,0},{2,1},{3,2},{4,7},{5,4},{6,5},{7,6},{8,11},{9,8},{10,9... | collective-permute-start | bytes 786440 | tf_op jit(solution)/shard_map/ppermute | solution.py:25
  14.9 17.5 %collective-permute-start.2 = (bf16[128,1024]{1,0:T(8,128)(2,1)}, bf16[128,1024]{1,0:T(8,128)(2,1)}, u32[]{:S(2)}, u32[]{:S(2)}) collective-permute-start(bf16[128,1024]{1,0:T(8,128)(2,1)} %get-tuple-element.49), channel_id=1, source_target_pairs={{0,1},{1,2},{2,3},{3,0},{4,5},{5,6},{6,7},{7,4},{8,9},{9,10},{10,1... | collective-permute-start | bytes 786440 | tf_op jit(solution)/shard_map/ppermute | solution.py:25
  35.6 15.5 %collective-permute-start.4 = (bf16[4,80,1024]{2,1,0:T(8,128)(2,1)}, bf16[4,80,1024]{2,1,0:T(8,128)(2,1)}, u32[]{:S(2)}, u32[]{:S(2)}) collective-permute-start(bf16[4,80,1024]{2,1,0:T(8,128)(2,1)} %broadcast_select_fusion.3), channel_id=1, source_target_pairs={{0,4},{1,5},{2,6},{3,7},{4,0},{5,1},{6,2},{7,3},{8,12},{9,13},{10,... | collective-permute-start | bytes 1966088 | tf_op jit(solution)/shard_map/ppermute | solution.py:25
  36.8 24.2 %collective-permute-start.8 = (bf16[128,1024]{1,0:T(8,128)(2,1)}, bf16[128,1024]{1,0:T(8,128)(2,1)S(1)}, u32[]{:S(2)}, u32[]{:S(2)}) collective-permute-start(bf16[128,1024]{1,0:T(8,128)(2,1)} %copy-done.15), channel_id=1, source_target_pairs={{0,2},{1,3},{2,0},{3,1},{4,6},{5,7},{6,4},{7,5},{8,10},{9,11},{10,... | collective-permute-start | bytes 786440 | tf_op jit(solution)/shard_map/ppermute | solution.py:25
  43.9 22.5 %collective-permute-start.9 = (bf16[128,1024]{1,0:T(8,128)(2,1)}, bf16[128,1024]{1,0:T(8,128)(2,1)S(1)}, u32[]{:S(2)}, u32[]{:S(2)}) collective-permute-start(bf16[128,1024]{1,0:T(8,128)(2,1)} %copy-done.14), channel_id=1, source_target_pairs={{0,3},{1,0},{2,1},{3,2},{4,7},{5,4},{6,5},{7,6},{8,11},{9,8},{10,9... | collective-permute-start | bytes 786440 | tf_op jit(solution)/shard_map/ppermute | solution.py:25
  44.3 22.1 %collective-permute-start.10 = (bf16[128,1024]{1,0:T(8,128)(2,1)}, bf16[128,1024]{1,0:T(8,128)(2,1)S(1)}, u32[]{:S(2)}, u32[]{:S(2)}) collective-permute-start(bf16[128,1024]{1,0:T(8,128)(2,1)} %copy-done.13), channel_id=1, source_target_pairs={{0,1},{1,2},{2,3},{3,0},{4,5},{5,6},{6,7},{7,4},{8,9},{9,10},{10,1... | collective-permute-start | bytes 786440 | tf_op jit(solution)/shard_map/ppermute | solution.py:25
  54.3 16.0 %collective-permute-start.7 = (bf16[2,80,1024]{2,1,0:T(8,128)(2,1)S(1)}, bf16[2,80,1024]{2,1,0:T(8,128)(2,1)S(1)}, u32[]{:S(2)}, u32[]{:S(2)}) collective-permute-start(bf16[2,80,1024]{2,1,0:T(8,128)(2,1)S(1)} %bitcast.178), channel_id=1, source_target_pairs={{0,3},{1,0},{2,1},{3,2},{4,7},{5,4},{6,5},{7,6},{8,11},{9,8},{10,9... | collective-permute-start | bytes 983048 | tf_op jit(solution)/shard_map/ppermute | solution.py:25
  58.1 21.9 %collective-permute-start.6 = (bf16[2,80,1024]{2,1,0:T(8,128)(2,1)S(1)}, bf16[2,80,1024]{2,1,0:T(8,128)(2,1)S(1)}, u32[]{:S(2)}, u32[]{:S(2)}) collective-permute-start(bf16[2,80,1024]{2,1,0:T(8,128)(2,1)S(1)} %bitcast.177), channel_id=1, source_target_pairs={{0,1},{1,2},{2,3},{3,0},{4,5},{5,6},{6,7},{7,4},{8,9},{9,10},{10,1... | collective-permute-start | bytes 983048 | tf_op jit(solution)/shard_map/ppermute | solution.py:25
  61.0 34.3 %collective-permute-start.5 = (bf16[2,80,1024]{2,1,0:T(8,128)(2,1)S(1)}, bf16[2,80,1024]{2,1,0:T(8,128)(2,1)S(1)}, u32[]{:S(2)}, u32[]{:S(2)}) collective-permute-start(bf16[2,80,1024]{2,1,0:T(8,128)(2,1)S(1)} %bitcast.176), channel_id=1, source_target_pairs={{0,2},{1,3},{2,0},{3,1},{4,6},{5,7},{6,4},{7,5},{8,10},{9,11},{10,... | collective-permute-start | bytes 983048 | tf_op jit(solution)/shard_map/ppermute | solution.py:25
  95.5 16.6 %collective-permute-start.13 = (bf16[4,80,1024]{2,1,0:T(8,128)(2,1)S(1)}, bf16[4,80,1024]{2,1,0:T(8,128)(2,1)S(1)}, u32[]{:S(2)}, u32[]{:S(2)}) collective-permute-start(bf16[4,80,1024]{2,1,0:T(8,128)(2,1)S(1)} %broadcast_select_fusion.1), channel_id=1, source_target_pairs={{0,4},{1,5},{2,6},{3,7},{4,0},{5,1},{6,2},{7,3},{8,12},{9,13},{10,... | collective-permute-start | bytes 1966088 | tf_op jit(solution)/shard_map/ppermute | solution.py:25
  97.8 19.7 %collective-permute-start.12 = (bf16[2,80,2048]{2,1,0:T(8,128)(2,1)S(1)}, bf16[2,80,2048]{2,1,0:T(8,128)(2,1)S(1)}, u32[]{:S(2)}, u32[]{:S(2)}) collective-permute-start(bf16[2,80,2048]{2,1,0:T(8,128)(2,1)S(1)} %pad_maximum_fusion.6), channel_id=1, source_target_pairs={{1,0},{2,1},{3,2},{5,4},{6,5},{7,6},{9,8},{10,9},{11,10},{13,12},{... | collective-permute-start | bytes 1966088 | tf_op jit(solution)/shard_map/ppermute | solution.py:25
  99.1 18.5 %collective-permute-start.11 = (bf16[2,80,2048]{2,1,0:T(8,128)(2,1)S(1)}, bf16[2,80,2048]{2,1,0:T(8,128)(2,1)S(1)}, u32[]{:S(2)}, u32[]{:S(2)}) collective-permute-start(bf16[2,80,2048]{2,1,0:T(8,128)(2,1)S(1)} %pad_maximum_fusion.6), channel_id=1, source_target_pairs={{0,1},{1,2},{2,3},{4,5},{5,6},{6,7},{8,9},{9,10},{10,11},{12,13},{... | collective-permute-start | bytes 1966088 | tf_op jit(solution)/shard_map/ppermute | solution.py:25
  117.5 27.3 %collective-permute-start.18 = (bf16[128,4096]{1,0:T(8,128)(2,1)S(1)}, bf16[128,4096]{1,0:T(8,128)(2,1)}, u32[]{:S(2)}, u32[]{:S(2)}) collective-permute-start(bf16[128,4096]{1,0:T(8,128)(2,1)S(1)} %bitcast.149), channel_id=1, source_target_pairs={{0,8},{1,9},{2,10},{3,11},{4,12},{5,13},{6,14},{7,15},{8,16},{9,17... | collective-permute-start | bytes 3145736 | tf_op jit(solution)/shard_map/ppermute | solution.py:25
  120.4 18.0 %collective-permute-start.16 = (bf16[2,80,2048]{2,1,0:T(8,128)(2,1)}, bf16[2,80,2048]{2,1,0:T(8,128)(2,1)}, u32[]{:S(2)}, u32[]{:S(2)}) collective-permute-start(bf16[2,80,2048]{2,1,0:T(8,128)(2,1)} %broadcast_select_fusion.5), channel_id=1, source_target_pairs={{0,1},{1,2},{2,3},{4,5},{5,6},{6,7},{8,9},{9,10},{10,11},{12,13},{... | collective-permute-start | bytes 1966088 | tf_op jit(solution)/shard_map/ppermute | solution.py:25
  125.4 19.5 %collective-permute-start.17 = (bf16[2,80,2048]{2,1,0:T(8,128)(2,1)}, bf16[2,80,2048]{2,1,0:T(8,128)(2,1)}, u32[]{:S(2)}, u32[]{:S(2)}) collective-permute-start(bf16[2,80,2048]{2,1,0:T(8,128)(2,1)} %broadcast_select_fusion), channel_id=1, source_target_pairs={{1,0},{2,1},{3,2},{5,4},{6,5},{7,6},{9,8},{10,9},{11,10},{13,12},{... | collective-permute-start | bytes 1966088 | tf_op jit(solution)/shard_map/ppermute | solution.py:25
  147.1 16.3 %collective-permute-start.19 = (bf16[2,80,2048]{2,1,0:T(8,128)(2,1)}, bf16[2,80,2048]{2,1,0:T(8,128)(2,1)}, u32[]{:S(2)}, u32[]{:S(2)}) collective-permute-start(bf16[2,80,2048]{2,1,0:T(8,128)(2,1)} %add_convert_fusion.3), channel_id=1, source_target_pairs={{0,1},{1,2},{2,3},{4,5},{5,6},{6,7},{8,9},{9,10},{10,11},{12,13},{... | collective-permute-start | bytes 1966088 | tf_op jit(solution)/shard_map/ppermute | solution.py:25
  149.4 21.5 %collective-permute-start.21 = (bf16[128,4096]{1,0:T(8,128)(2,1)S(1)}, bf16[128,4096]{1,0:T(8,128)(2,1)}, u32[]{:S(2)}, u32[]{:S(2)}) collective-permute-start(bf16[128,4096]{1,0:T(8,128)(2,1)S(1)} %bitcast.151), channel_id=1, source_target_pairs={{0,24},{1,25},{2,26},{3,27},{4,28},{5,29},{6,30},{7,31},{8,0},{9,1... | collective-permute-start | bytes 3145736 | tf_op jit(solution)/shard_map/ppermute | solution.py:25
  151.6 19.3 %collective-permute-start.20 = (bf16[2,80,2048]{2,1,0:T(8,128)(2,1)}, bf16[2,80,2048]{2,1,0:T(8,128)(2,1)}, u32[]{:S(2)}, u32[]{:S(2)}) collective-permute-start(bf16[2,80,2048]{2,1,0:T(8,128)(2,1)} %add_convert_fusion.2), channel_id=1, source_target_pairs={{1,0},{2,1},{3,2},{5,4},{6,5},{7,6},{9,8},{10,9},{11,10},{13,12},{... | collective-permute-start | bytes 1966088 | tf_op jit(solution)/shard_map/ppermute | solution.py:25
  173.6 18.3 %collective-permute-start.23 = (bf16[2,80,2048]{2,1,0:T(8,128)(2,1)S(1)}, bf16[2,80,2048]{2,1,0:T(8,128)(2,1)S(1)}, u32[]{:S(2)}, u32[]{:S(2)}) collective-permute-start(bf16[2,80,2048]{2,1,0:T(8,128)(2,1)S(1)} %add_convert_fusion), channel_id=1, source_target_pairs={{1,0},{2,1},{3,2},{5,4},{6,5},{7,6},{9,8},{10,9},{11,10},{13,12},{... | collective-permute-start | bytes 1966088 | tf_op jit(solution)/shard_map/ppermute | solution.py:25
  175.1 18.1 %collective-permute-start.22 = (bf16[2,80,2048]{2,1,0:T(8,128)(2,1)S(1)}, bf16[2,80,2048]{2,1,0:T(8,128)(2,1)S(1)}, u32[]{:S(2)}, u32[]{:S(2)}) collective-permute-start(bf16[2,80,2048]{2,1,0:T(8,128)(2,1)S(1)} %add_convert_fusion.1), channel_id=1, source_target_pairs={{0,1},{1,2},{2,3},{4,5},{5,6},{6,7},{8,9},{9,10},{10,11},{12,13},{... | collective-permute-start | bytes 1966088 | tf_op jit(solution)/shard_map/ppermute | solution.py:25
  186.4 15.8 %collective-permute-start.27 = (bf16[4,80,1024]{2,1,0:T(8,128)(2,1)S(1)}, bf16[4,80,1024]{2,1,0:T(8,128)(2,1)S(1)}, u32[]{:S(2)}, u32[]{:S(2)}) collective-permute-start(bf16[4,80,1024]{2,1,0:T(8,128)(2,1)S(1)} %dynamic-slice_bitcast_fusion.1), channel_id=1, source_target_pairs={{0,4},{1,5},{2,6},{3,7},{4,0},{5,1},{6,2},{7,3},{8,12},{9,13},{10,... | collective-permute-start | bytes 1966088 | tf_op jit(solution)/shard_map/ppermute | solution.py:25
  193.6 25.1 %collective-permute-start.25 = (bf16[2,80,1024]{2,1,0:T(8,128)(2,1)S(1)}, bf16[2,80,1024]{2,1,0:T(8,128)(2,1)S(1)}, u32[]{:S(2)}, u32[]{:S(2)}) collective-permute-start(bf16[2,80,1024]{2,1,0:T(8,128)(2,1)S(1)} %fusion.30), channel_id=1, source_target_pairs={{0,2},{1,3},{2,0},{3,1},{4,6},{5,7},{6,4},{7,5},{8,10},{9,11},{10,... | collective-permute-start | bytes 983048 | tf_op jit(solution)/shard_map/ppermute | solution.py:25
  195.9 22.9 %collective-permute-start.24 = (bf16[2,80,1024]{2,1,0:T(8,128)(2,1)S(1)}, bf16[2,80,1024]{2,1,0:T(8,128)(2,1)S(1)}, u32[]{:S(2)}, u32[]{:S(2)}) collective-permute-start(bf16[2,80,1024]{2,1,0:T(8,128)(2,1)S(1)} %fusion.30), channel_id=1, source_target_pairs={{0,3},{1,0},{2,1},{3,2},{4,7},{5,4},{6,5},{7,6},{8,11},{9,8},{10,9... | collective-permute-start | bytes 983048 | tf_op jit(solution)/shard_map/ppermute | solution.py:25
  198.6 20.2 %collective-permute-start.26 = (bf16[2,80,1024]{2,1,0:T(8,128)(2,1)S(1)}, bf16[2,80,1024]{2,1,0:T(8,128)(2,1)S(1)}, u32[]{:S(2)}, u32[]{:S(2)}) collective-permute-start(bf16[2,80,1024]{2,1,0:T(8,128)(2,1)S(1)} %fusion.30), channel_id=1, source_target_pairs={{0,1},{1,2},{2,3},{3,0},{4,5},{5,6},{6,7},{7,4},{8,9},{9,10},{10,1... | collective-permute-start | bytes 983048 | tf_op jit(solution)/shard_map/ppermute | solution.py:25
  222.2 20.8 %collective-permute-start.35 = (bf16[128,1024]{1,0:T(8,128)(2,1)S(1)}, bf16[128,1024]{1,0:T(8,128)(2,1)S(1)}, u32[]{:S(2)}, u32[]{:S(2)}) collective-permute-start(bf16[128,1024]{1,0:T(8,128)(2,1)S(1)} %get-tuple-element.118), channel_id=1, source_target_pairs={{0,27},{1,24},{2,25},{3,26},{4,31},{5,28},{6,29},{7,30},{8,3},{9,0... | collective-permute-start | bytes 786440 | tf_op jit(solution)/shard_map/ppermute | solution.py:25
  223.2 36.7 %collective-permute-start.34 = (bf16[128,1024]{1,0:T(8,128)(2,1)S(1)}, bf16[128,1024]{1,0:T(8,128)(2,1)S(1)}, u32[]{:S(2)}, u32[]{:S(2)}) collective-permute-start(bf16[128,1024]{1,0:T(8,128)(2,1)S(1)} %get-tuple-element.119), channel_id=1, source_target_pairs={{0,25},{1,26},{2,27},{3,24},{4,29},{5,30},{6,31},{7,28},{8,1},{9,2... | collective-permute-start | bytes 786440 | tf_op jit(solution)/shard_map/ppermute | solution.py:25
  227.2 36.8 %collective-permute-start.33 = (bf16[128,1024]{1,0:T(8,128)(2,1)}, bf16[128,1024]{1,0:T(8,128)(2,1)S(1)}, u32[]{:S(2)}, u32[]{:S(2)}) collective-permute-start(bf16[128,1024]{1,0:T(8,128)(2,1)} %get-tuple-element.120), channel_id=1, source_target_pairs={{0,26},{1,27},{2,24},{3,25},{4,30},{5,31},{6,28},{7,29},{8,2},{9,3... | collective-permute-start | bytes 786440 | tf_op jit(solution)/shard_map/ppermute | solution.py:25
  235.9 31.3 %collective-permute-start.32 = (bf16[128,1024]{1,0:T(8,128)(2,1)}, bf16[128,1024]{1,0:T(8,128)(2,1)}, u32[]{:S(2)}, u32[]{:S(2)}) collective-permute-start(bf16[128,1024]{1,0:T(8,128)(2,1)} %get-tuple-element.109), channel_id=1, source_target_pairs={{0,8},{1,9},{2,10},{3,11},{4,12},{5,13},{6,14},{7,15},{8,16},{9,17... | collective-permute-start | bytes 786440 | tf_op jit(solution)/shard_map/ppermute | solution.py:25
  235.9 31.3 %collective-permute-start.29 = (bf16[128,1024]{1,0:T(8,128)(2,1)}, bf16[128,1024]{1,0:T(8,128)(2,1)}, u32[]{:S(2)}, u32[]{:S(2)}) collective-permute-start(bf16[128,1024]{1,0:T(8,128)(2,1)} %get-tuple-element.110), channel_id=1, source_target_pairs={{0,10},{1,11},{2,8},{3,9},{4,14},{5,15},{6,12},{7,13},{8,18},{9,19... | collective-permute-start | bytes 786440 | tf_op jit(solution)/shard_map/ppermute | solution.py:25
  243.1 24.1 %collective-permute-start.30 = (bf16[128,1024]{1,0:T(8,128)(2,1)}, bf16[128,1024]{1,0:T(8,128)(2,1)}, u32[]{:S(2)}, u32[]{:S(2)}) collective-permute-start(bf16[128,1024]{1,0:T(8,128)(2,1)} %get-tuple-element.111), channel_id=1, source_target_pairs={{0,9},{1,10},{2,11},{3,8},{4,13},{5,14},{6,15},{7,12},{8,17},{9,18... | collective-permute-start | bytes 786440 | tf_op jit(solution)/shard_map/ppermute | solution.py:25
  (38 other events, 360.3 us)
